TPU v7x, 32 devices: a whole 2x2x4 slice. The times are simulated.
32 devices in a mesh: groups: 2 (over y), kv: 16 (over z, x, core).
Axes of the slice: x: 2, y: 2, z: 4, core: 2. Of those that a mesh axis runs over, the one named last changes fastest.
Arguments:
- queries: bfloat16 [2, 1024, 4096], P(None, ('groups', 'kv')), parts along dimension 1, as said below
- shared_prefix_keys: bfloat16 [16384, 512], P('kv'), may hold values from -6 to 6
- shared_prefix_values: bfloat16 [16384, 512], P('kv'), may hold values from -6 to 6
- row_suffix_keys: bfloat16 [1024, 32, 512], P(('groups', 'kv')), parts along dimension 0, may hold values from -6 to 6
- row_suffix_values: bfloat16 [1024, 32, 512], P(('groups', 'kv')), parts along dimension 0, may hold values from -6 to 6
- step_keys: bfloat16 [2, 1024, 512], P(None, ('groups', 'kv')), parts along dimension 1, may hold values from -6 to 6
- step_values: bfloat16 [2, 1024, 512], P(None, ('groups', 'kv')), parts along dimension 1, may hold values from -6 to 6
- tree_blocks: int32 [1024, 4], P(('groups', 'kv')), parts along dimension 0, may hold values from 0 to 15, all different within a row; in each aligned block of 32 rows (0 to 31, 32 to 63, ...) at most 16 rows name the same one
- block_slot: int32 [16], replicated, may hold values from 0 to 15, each once
- suffix_length: int32 [1024], P(('groups', 'kv')), parts along dimension 0, may hold values from 1 to 32, as said below
Outputs:
- attended: bfloat16 [2, 1024, 4096], P(None, ('groups', 'kv')), parts along dimension 1
There are 2 independent parts, one for each index of `groups`. A program takes and returns all parts, laid end to end along the dimension named above; an argument that names none is the same for every part. Nothing has to cross between parts.
Inputs may be any that keep to these rules, and one draw needn't show every extreme that they name: `tree_blocks`: each row lists 4 different tree blocks; among the rows of one kv index no block is listed by more than 16 rows, and some block by exactly 16. A permutation: tree block b lies in slot block_slot[b]. `suffix_length`: some row holds 32 cached positions and some row one. Real-valued queries.
All inputs are finite; a program needn't handle non-finite values.
Results may differ from a plain program's by a relative error of at most 0.0057.
Values may be sent and summed in bfloat16 or wider, within the bound.
A program may use at most 128 MiB of HBM per device.

v0:
```python
import math

import jax
import jax.numpy as jnp
from jax import lax
from jax.sharding import PartitionSpec as P

QUERY_HEADS = 32
KEY_VALUE_HEADS = 4
HEAD_SIZE = 128
BLOCK_TOKENS = 1024
PATH_BLOCKS = 4
SUFFIX_SLOTS = 32
DECODE_STEPS = 2


NEG = -1e30


def heads_first(block_table):
    return block_table.reshape(BLOCK_TOKENS, KEY_VALUE_HEADS, HEAD_SIZE).transpose(1, 0, 2)


def head_partial(operand_list):
    query_rows, key_rows, value_rows = operand_list
    scores = lax.dot_general(
        query_rows, key_rows, (((1,), (1,)), ((), ())), preferred_element_type=jnp.float32
    ) / math.sqrt(HEAD_SIZE)
    running_maximum = jnp.max(scores, axis=1)
    expon = jnp.exp(scores - running_maximum[:, None])
    running_total = jnp.sum(expon, axis=1)
    weights = expon.astype(jnp.bfloat16)
    mixed_output = (
        jnp.dot(weights, value_rows, preferred_element_type=jnp.float32) / running_total[:, None]
    )
    return (mixed_output.astype(jnp.bfloat16), running_maximum, running_total)


def attend_block(tile_list, key_heads, value_heads):
    head_group = QUERY_HEADS // KEY_VALUE_HEADS
    sender_list = tile_list.shape[0]
    entry_list = tile_list.shape[1]
    row_count = sender_list * entry_list
    grouped = (
        tile_list.reshape(row_count, KEY_VALUE_HEADS, head_group, HEAD_SIZE)
        .transpose(1, 0, 2, 3)
        .reshape(KEY_VALUE_HEADS, row_count * head_group, HEAD_SIZE)
    )
    mixed_output, running_maximum, running_total = lax.map(
        head_partial, (grouped, key_heads, value_heads)
    )
    mixed_output = (
        mixed_output.reshape(KEY_VALUE_HEADS, row_count, head_group, HEAD_SIZE)
        .transpose(1, 0, 2, 3)
        .reshape(sender_list, entry_list, QUERY_HEADS * HEAD_SIZE)
    )
    running_maximum = (
        running_maximum.reshape(KEY_VALUE_HEADS, row_count, head_group)
        .transpose(1, 0, 2)
        .reshape(sender_list, entry_list, QUERY_HEADS)
    )
    running_total = (
        running_total.reshape(KEY_VALUE_HEADS, row_count, head_group)
        .transpose(1, 0, 2)
        .reshape(sender_list, entry_list, QUERY_HEADS)
    )
    return (mixed_output, running_maximum, running_total)


def own_partial(
    query_head_rows,
    cached_key_rows,
    cached_value_rows,
    latest_keys,
    latest_values,
    lengths,
    step_index,
):
    first = jnp.einsum(
        "bhgd,bkhd->bhgk", query_head_rows, cached_key_rows, preferred_element_type=jnp.float32
    ) / math.sqrt(HEAD_SIZE)
    valid = (
        jnp.arange(SUFFIX_SLOTS, dtype=jnp.int32)[None, None, None, :]
        < lengths[:, None, None, None]
    )
    first = jnp.where(valid, first, NEG)
    second = jnp.einsum(
        "bhgd,sbhd->bhgs", query_head_rows, latest_keys, preferred_element_type=jnp.float32
    ) / math.sqrt(HEAD_SIZE)
    second = jnp.where(
        jnp.arange(DECODE_STEPS, dtype=jnp.int32)[None, None, None, :] <= step_index, second, NEG
    )
    scores = jnp.concatenate([first, second], axis=-1)
    running_maximum = jnp.max(scores, axis=-1)
    expon = jnp.exp(scores - running_maximum[..., None])
    running_total = jnp.sum(expon, axis=-1)
    weights = expon.astype(jnp.bfloat16)
    mixed_output = jnp.einsum(
        "bhgk,bkhd->bhgd",
        weights[..., :SUFFIX_SLOTS],
        cached_value_rows,
        preferred_element_type=jnp.float32,
    )
    mixed_output = mixed_output + jnp.einsum(
        "bhgs,sbhd->bhgd",
        weights[..., SUFFIX_SLOTS:],
        latest_values,
        preferred_element_type=jnp.float32,
    )
    return (running_maximum, running_total, mixed_output / running_total[..., None])


def merge_parts(own_top, own_total, own_mixed, path_top, path_total, path_mixed):
    running_maximum = jnp.maximum(own_top, jnp.max(path_top, axis=1))
    own_factor = own_total * jnp.exp(own_top - running_maximum)
    path_factor = path_total * jnp.exp(path_top - running_maximum[:, None])
    numer = own_factor[..., None] * own_mixed + jnp.sum(path_factor[..., None] * path_mixed, axis=1)
    denom = own_factor + jnp.sum(path_factor, axis=1)
    result = numer / denom[..., None]
    return result.reshape(result.shape[0], QUERY_HEADS * HEAD_SIZE).astype(jnp.bfloat16)


def per_device(
    queries,
    shared_prefix_keys,
    shared_prefix_values,
    row_suffix_keys,
    row_suffix_values,
    step_keys,
    step_values,
    tree_blocks,
    block_slot,
    suffix_length,
):
    head_group = QUERY_HEADS // KEY_VALUE_HEADS
    devices = lax.axis_size("kv")
    row_indices = queries.shape[1]
    capacity = max(2, 2 * row_indices * PATH_BLOCKS // devices)
    slots_all = devices * capacity
    blocks_flat = tree_blocks.reshape(-1)
    device_ids = jnp.arange(devices, dtype=jnp.int32)
    target = jnp.sum(
        jnp.where(blocks_flat[:, None] == device_ids[None, :], block_slot[None, :], 0), axis=1
    )
    own_keys = heads_first(shared_prefix_keys)
    own_values = heads_first(shared_prefix_values)
    hits = (target[:, None] == device_ids[None, :]).astype(jnp.int32)
    before = jnp.cumsum(hits, axis=0) - hits
    rank = jnp.sum(before * hits, axis=1)
    slot_index = target * capacity + rank
    placing = (slot_index[:, None] == jnp.arange(slots_all, dtype=jnp.int32)[None, :]).astype(
        jnp.bfloat16
    )
    placing_wide = placing.astype(jnp.float32)
    per_row = jnp.sum(placing.reshape(row_indices, PATH_BLOCKS, slots_all), axis=1)
    cached_key_rows = row_suffix_keys.reshape(row_indices, SUFFIX_SLOTS, KEY_VALUE_HEADS, HEAD_SIZE)
    cached_value_rows = row_suffix_values.reshape(
        row_indices, SUFFIX_SLOTS, KEY_VALUE_HEADS, HEAD_SIZE
    )
    latest_keys = step_keys.reshape(DECODE_STEPS, row_indices, KEY_VALUE_HEADS, HEAD_SIZE)
    latest_values = step_values.reshape(DECODE_STEPS, row_indices, KEY_VALUE_HEADS, HEAD_SIZE)
    outputs = []
    for step_index in range(DECODE_STEPS):
        step_query = queries[step_index]
        sending = lax.dot_general(
            per_row, step_query, (((0,), (0,)), ((), ())), preferred_element_type=jnp.float32
        )
        sending = sending.astype(jnp.bfloat16).reshape(devices, capacity, QUERY_HEADS * HEAD_SIZE)
        results = attend_block(
            lax.all_to_all(sending, "kv", split_axis=0, concat_axis=0, tiled=True),
            own_keys,
            own_values,
        )
        mixed_back = lax.all_to_all(
            results[0].astype(jnp.float32), "kv", split_axis=0, concat_axis=0, tiled=True
        ).astype(jnp.bfloat16)
        top_back = lax.all_to_all(results[1], "kv", split_axis=0, concat_axis=0, tiled=True)
        total_back = lax.all_to_all(results[2], "kv", split_axis=0, concat_axis=0, tiled=True)
        tile_mixed_output = jnp.dot(
            placing,
            mixed_back.reshape(slots_all, QUERY_HEADS * HEAD_SIZE),
            preferred_element_type=jnp.float32,
        )
        tile_maximum = jnp.dot(
            placing_wide, top_back.reshape(slots_all, QUERY_HEADS), precision=lax.Precision.HIGHEST
        )
        tile_denominator = jnp.dot(
            placing_wide,
            total_back.reshape(slots_all, QUERY_HEADS),
            precision=lax.Precision.HIGHEST,
        )
        query_head_rows = step_query.reshape(row_indices, KEY_VALUE_HEADS, head_group, HEAD_SIZE)
        own_top, own_total, own_mixed = own_partial(
            query_head_rows,
            cached_key_rows,
            cached_value_rows,
            latest_keys,
            latest_values,
            suffix_length,
            step_index,
        )
        outputs.append(
            merge_parts(
                own_top,
                own_total,
                own_mixed,
                tile_maximum.reshape(row_indices, PATH_BLOCKS, KEY_VALUE_HEADS, head_group),
                tile_denominator.reshape(row_indices, PATH_BLOCKS, KEY_VALUE_HEADS, head_group),
                tile_mixed_output.reshape(
                    row_indices, PATH_BLOCKS, KEY_VALUE_HEADS, head_group, HEAD_SIZE
                ),
            )
        )
    return jnp.stack(outputs)


def solution(mesh):
    return jax.shard_map(
        per_device,
        mesh=mesh,
        in_specs=(
            P(None, ("groups", "kv"), None),
            P("kv", None),
            P("kv", None),
            P(("groups", "kv"), None, None),
            P(("groups", "kv"), None, None),
            P(None, ("groups", "kv"), None),
            P(None, ("groups", "kv"), None),
            P(("groups", "kv"), None),
            P(),
            P(("groups", "kv")),
        ),
        out_specs=P(None, ("groups", "kv"), None),
        check_vma=False,
    )
```

profile of v0, /device:TPU:11, one launch (start us, length us, event | category | flops | bytes accessed | tf_op | source)
XLA Modules:
  0.0 313.8 jit_solution(15994195184654716173)
XLA Ops:
  5.6 6.7 %all-to-all-start = ((bf16[16,16,4096]{2,1,0:T(8,128)(2,1)}), bf16[16,16,4096]{2,1,0:T(8,128)(2,1)}, u32[]{:S(2)}, u32[]{:S(2)}) async-start(bf16[16,16,4096]{2,1,0:T(8,128)(2,1)} %bitcast.16), calls=%async_computation | async-start | bytes 4194304 | tf_op jit(solution)/shard_map/all_to_all | solution.py:170
  19.3 40.5 %all-to-all-done = bf16[16,16,4096]{2,1,0:T(8,128)(2,1)} async-done(((bf16[16,16,4096]{2,1,0:T(8,128)(2,1)}), bf16[16,16,4096]{2,1,0:T(8,128)(2,1)}, u32[]{:S(2)}, u32[]{:S(2)}) %all-to-all-start) | async-done | bytes 2097184 | tf_op jit(solution)/shard_map/all_to_all | solution.py:170
  59.8 4.9 %all-to-all-start.4 = ((bf16[16,16,4096]{2,1,0:T(8,128)(2,1)}), bf16[16,16,4096]{2,1,0:T(8,128)(2,1)}, u32[]{:S(2)}, u32[]{:S(2)}) async-start(bf16[16,16,4096]{2,1,0:T(8,128)(2,1)} %bitcast.255), calls=%async_computation.4 | async-start | bytes 4194304 | tf_op jit(solution)/shard_map/all_to_all | solution.py:170
  70.1 29.6 %while.28 = (s32[]{:T(128)}, bf16[4,2048,128]{2,1,0:T(8,128)(2,1)}, f32[4,2048]{1,0:T(4,128)S(1)}, f32[4,2048]{1,0:T(4,128)S(1)}, bf16[4,2048,128]{2,1,0:T(8,128...) while((s32[]{:T(128)}, bf16[4,2048,128]{2,1,0:T(8,128)(2,1)}, ...), condition=%wide.region_10.11_spmd, body=%wide.region_7.10_spmd.sunk | while | flops 1091039232 | bytes 26814564 | solution.py:49
  73.8 3.4 %fusion.158 = bf16[4,2048,128]{2,1,0:T(8,128)(2,1)} fusion(bf16[4,2048,128]{2,1,0:T(8,128)(2,1)} %get-tuple-element.352, s32[]{:T(128)} %get-tuple-element.351, f32[2048,1024]{0,1:T(8,128)S(1)} %get-tuple-element.304, f32[2048]{0:T(1024)S(1)} %get-tuple-element.305, f32[2048]{0:T(1024)S(1)} %fusion.157, bf16[4,1024,128]{2,1,0:T(8,128)(2,1)} %get-tuple-element.366), kind=kOutput, calls=%fused_computation.10.clone.1 | convolution fusion | flops 543686656 | bytes 9192448 | tf_op jit(solution)/shard_map/while/body/eval_jaxpr/dot_general | solution.py:34
  81.2 3.4 %fusion.158 = bf16[4,2048,128]{2,1,0:T(8,128)(2,1)} fusion(bf16[4,2048,128]{2,1,0:T(8,128)(2,1)} %get-tuple-element.352, s32[]{:T(128)} %get-tuple-element.351, f32[2048,1024]{0,1:T(8,128)S(1)} %get-tuple-element.304, f32[2048]{0:T(1024)S(1)} %get-tuple-element.305, f32[2048]{0:T(1024)S(1)} %fusion.157, bf16[4,1024,128]{2,1,0:T(8,128)(2,1)} %get-tuple-element.366), kind=kOutput, calls=%fused_computation.10.clone.1 | convolution fusion | flops 543686656 | bytes 9192448 | tf_op jit(solution)/shard_map/while/body/eval_jaxpr/dot_general | solution.py:34
  88.6 3.4 %fusion.158 = bf16[4,2048,128]{2,1,0:T(8,128)(2,1)} fusion(bf16[4,2048,128]{2,1,0:T(8,128)(2,1)} %get-tuple-element.352, s32[]{:T(128)} %get-tuple-element.351, f32[2048,1024]{0,1:T(8,128)S(1)} %get-tuple-element.304, f32[2048]{0:T(1024)S(1)} %get-tuple-element.305, f32[2048]{0:T(1024)S(1)} %fusion.157, bf16[4,1024,128]{2,1,0:T(8,128)(2,1)} %get-tuple-element.366), kind=kOutput, calls=%fused_computation.10.clone.1 | convolution fusion | flops 543686656 | bytes 9192448 | tf_op jit(solution)/shard_map/while/body/eval_jaxpr/dot_general | solution.py:34
  96.0 3.4 %fusion.158 = bf16[4,2048,128]{2,1,0:T(8,128)(2,1)} fusion(bf16[4,2048,128]{2,1,0:T(8,128)(2,1)} %get-tuple-element.352, s32[]{:T(128)} %get-tuple-element.351, f32[2048,1024]{0,1:T(8,128)S(1)} %get-tuple-element.304, f32[2048]{0:T(1024)S(1)} %get-tuple-element.305, f32[2048]{0:T(1024)S(1)} %fusion.157, bf16[4,1024,128]{2,1,0:T(8,128)(2,1)} %get-tuple-element.366), kind=kOutput, calls=%fused_computation.10.clone.1 | convolution fusion | flops 543686656 | bytes 9192448 | tf_op jit(solution)/shard_map/while/body/eval_jaxpr/dot_general | solution.py:34
  101.2 11.0 %all-to-all-done.4 = bf16[16,16,4096]{2,1,0:T(8,128)(2,1)} async-done(((bf16[16,16,4096]{2,1,0:T(8,128)(2,1)}), bf16[16,16,4096]{2,1,0:T(8,128)(2,1)}, u32[]{:S(2)}, u32[]{:S(2)}) %all-to-all-start.4) | async-done | bytes 2097184 | tf_op jit(solution)/shard_map/all_to_all | solution.py:170
  112.2 4.9 %all-to-all-start.1 = ((f32[16,1,512]{2,1,0:T(1,128)}), f32[16,1,512]{2,1,0:T(1,128)S(1)}, u32[]{:S(2)}, u32[]{:S(2)}) async-start(f32[16,1,512]{2,1,0:T(1,128)} %reshape.395), calls=%async_computation.1 | async-start | bytes 65536 | tf_op jit(solution)/shard_map/all_to_all | solution.py:177
  122.4 6.0 %all-to-all-start.2 = ((f32[16,1,512]{2,1,0:T(1,128)}), f32[16,1,512]{2,1,0:T(1,128)}, u32[]{:S(2)}, u32[]{:S(2)}) async-start(f32[16,1,512]{2,1,0:T(1,128)} %reshape.397), calls=%async_computation.2 | async-start | bytes 65536 | tf_op jit(solution)/shard_map/all_to_all | solution.py:178
  130.7 34.6 %while.29 = (s32[]{:T(128)}, bf16[4,2048,128]{2,1,0:T(8,128)(2,1)}, f32[4,2048]{1,0:T(4,128)S(1)}, f32[4,2048]{1,0:T(4,128)}, bf16[4,2048,128]{2,1,0:T(8,128)(2,...) while((s32[]{:T(128)}, bf16[4,2048,128]{2,1,0:T(8,128)(2,1)}, ...), condition=%wide.region_20.21_spmd, body=%wide.region_17.20_spmd.sunk | while | flops 1091039232 | bytes 26814564 | solution.py:49
  134.4 3.4 %fusion.162 = bf16[4,2048,128]{2,1,0:T(8,128)(2,1)} fusion(bf16[4,2048,128]{2,1,0:T(8,128)(2,1)} %get-tuple-element.325, s32[]{:T(128)} %get-tuple-element.324, f32[2048,1024]{0,1:T(8,128)S(1)} %get-tuple-element.313, f32[2048]{0:T(1024)S(1)} %get-tuple-element.314, f32[2048]{0:T(1024)S(1)} %fusion.161, bf16[4,1024,128]{2,1,0:T(8,128)(2,1)} %get-tuple-element.339), kind=kOutput, calls=%fused_computation.31.clone.1 | convolution fusion | flops 543686656 | bytes 9192448 | tf_op jit(solution)/shard_map/while/body/eval_jaxpr/dot_general | solution.py:34
  143.0 3.4 %fusion.162 = bf16[4,2048,128]{2,1,0:T(8,128)(2,1)} fusion(bf16[4,2048,128]{2,1,0:T(8,128)(2,1)} %get-tuple-element.325, s32[]{:T(128)} %get-tuple-element.324, f32[2048,1024]{0,1:T(8,128)S(1)} %get-tuple-element.313, f32[2048]{0:T(1024)S(1)} %get-tuple-element.314, f32[2048]{0:T(1024)S(1)} %fusion.161, bf16[4,1024,128]{2,1,0:T(8,128)(2,1)} %get-tuple-element.339), kind=kOutput, calls=%fused_computation.31.clone.1 | convolution fusion | flops 543686656 | bytes 9192448 | tf_op jit(solution)/shard_map/while/body/eval_jaxpr/dot_general | solution.py:34
  151.7 3.4 %fusion.162 = bf16[4,2048,128]{2,1,0:T(8,128)(2,1)} fusion(bf16[4,2048,128]{2,1,0:T(8,128)(2,1)} %get-tuple-element.325, s32[]{:T(128)} %get-tuple-element.324, f32[2048,1024]{0,1:T(8,128)S(1)} %get-tuple-element.313, f32[2048]{0:T(1024)S(1)} %get-tuple-element.314, f32[2048]{0:T(1024)S(1)} %fusion.161, bf16[4,1024,128]{2,1,0:T(8,128)(2,1)} %get-tuple-element.339), kind=kOutput, calls=%fused_computation.31.clone.1 | convolution fusion | flops 543686656 | bytes 9192448 | tf_op jit(solution)/shard_map/while/body/eval_jaxpr/dot_general | solution.py:34
  160.4 3.4 %fusion.162 = bf16[4,2048,128]{2,1,0:T(8,128)(2,1)} fusion(bf16[4,2048,128]{2,1,0:T(8,128)(2,1)} %get-tuple-element.325, s32[]{:T(128)} %get-tuple-element.324, f32[2048,1024]{0,1:T(8,128)S(1)} %get-tuple-element.313, f32[2048]{0:T(1024)S(1)} %get-tuple-element.314, f32[2048]{0:T(1024)S(1)} %fusion.161, bf16[4,1024,128]{2,1,0:T(8,128)(2,1)} %get-tuple-element.339), kind=kOutput, calls=%fused_computation.31.clone.1 | convolution fusion | flops 543686656 | bytes 9192448 | tf_op jit(solution)/shard_map/while/body/eval_jaxpr/dot_general | solution.py:34
  168.7 6.0 %all-to-all-start.5 = ((f32[16,1,512]{2,1,0:T(1,128)}), f32[16,1,512]{2,1,0:T(1,128)}, u32[]{:S(2)}, u32[]{:S(2)}) async-start(f32[16,1,512]{2,1,0:T(1,128)} %reshape.391), calls=%async_computation.5 | async-start | bytes 65536 | tf_op jit(solution)/shard_map/all_to_all | solution.py:177
  179.0 5.9 %all-to-all-start.6 = ((f32[16,1,512]{2,1,0:T(1,128)}), f32[16,1,512]{2,1,0:T(1,128)S(1)}, u32[]{:S(2)}, u32[]{:S(2)}) async-start(f32[16,1,512]{2,1,0:T(1,128)} %reshape.393), calls=%async_computation.6 | async-start | bytes 65536 | tf_op jit(solution)/shard_map/all_to_all | solution.py:178
  186.6 4.2 %reshape.379 = bf16[16,16,4096]{2,1,0:T(8,128)(2,1)} reshape(bf16[256,4,8,128]{3,2,1,0:T(8,128)(2,1)} %copy_bitcast_fusion.1) | data formatting | bytes 4194304 | tf_op jit(solution)/shard_map/convert_element_type | solution.py:175
  191.4 6.1 %all-to-all-start.3 = ((bf16[16,16,4096]{2,1,0:T(8,128)(2,1)}), bf16[16,16,4096]{2,1,0:T(8,128)(2,1)S(1)}, u32[]{:S(2)}, u32[]{:S(2)}) async-start(bf16[16,16,4096]{2,1,0:T(8,128)(2,1)} %reshape.379), calls=%async_computation.3 | async-start | bytes 4194304 | tf_op jit(solution)/shard_map/all_to_all | solution.py:174
  206.7 4.2 %reshape.380 = bf16[16,16,4096]{2,1,0:T(8,128)(2,1)} reshape(bf16[256,4,8,128]{3,2,1,0:T(8,128)(2,1)} %copy_bitcast_fusion) | data formatting | bytes 4194304 | tf_op jit(solution)/shard_map/convert_element_type | solution.py:175
  210.9 34.0 %all-to-all-done.3 = bf16[16,16,4096]{2,1,0:T(8,128)(2,1)S(1)} async-done(((bf16[16,16,4096]{2,1,0:T(8,128)(2,1)}), bf16[16,16,4096]{2,1,0:T(8,128)(2,1)S(1)}, u32[]{:S(2)}, u32[]{:S(2)}) %all-to-all-start.3) | async-done | bytes 2097184 | tf_op jit(solution)/shard_map/all_to_all | solution.py:174
  244.8 4.9 %all-to-all-start.7 = ((bf16[16,16,4096]{2,1,0:T(8,128)(2,1)}), bf16[16,16,4096]{2,1,0:T(8,128)(2,1)}, u32[]{:S(2)}, u32[]{:S(2)}) async-start(bf16[16,16,4096]{2,1,0:T(8,128)(2,1)} %reshape.380), calls=%async_computation.7 | async-start | bytes 4194304 | tf_op jit(solution)/shard_map/all_to_all | solution.py:174
  307.3 3.3 %copy.260 = bf16[4096,256]{1,0:T(8,128)(2,1)S(1)} copy(bf16[4096,256]{0,1:T(8,128)(2,1)} %bitcast.63) | data formatting | bytes 4194304 | tf_op jit(solution)/shard_map/dot_general | solution.py:179
  (188 shorter events, 143.1 us)
Async XLA Ops:
  0.0 306.5 %copy-start = (bf16[32,32,512]{2,1,0:T(8,128)(2,1)S(1)}, bf16[32,32,512]{2,1,0:T(8,128)(2,1)}, u32[]{:S(2)}) copy-start(bf16[32,32,512]{2,1,0:T(8,128)(2,1)} %param.18) | copy-start | bytes 3145732
  2.4 259.7 %copy-start.13 = (s32[32,4]{0,1:T(4,128)}, s32[32,4]{0,1:T(4,128)S(1)}, u32[]{:S(2)}) copy-start(s32[32,4]{0,1:T(4,128)S(1)} %copy.217) | copy-start | bytes 1540
  5.6 6.7 %copy-start.3 = (bf16[1024,512]{1,0:T(8,128)(2,1)S(1)}, bf16[1024,512]{1,0:T(8,128)(2,1)}, u32[]{:S(2)}) copy-start(bf16[1024,512]{1,0:T(8,128)(2,1)} %param.15) | copy-start | bytes 3145732
  5.6 54.2 %all-to-all-start = ((bf16[16,16,4096]{2,1,0:T(8,128)(2,1)}), bf16[16,16,4096]{2,1,0:T(8,128)(2,1)}, u32[]{:S(2)}, u32[]{:S(2)}) async-start(bf16[16,16,4096]{2,1,0:T(8,128)(2,1)} %bitcast.16), calls=%async_computation | async-start | bytes 4194304 | tf_op jit(solution)/shard_map/all_to_all | solution.py:170
  59.8 52.4 %all-to-all-start.4 = ((bf16[16,16,4096]{2,1,0:T(8,128)(2,1)}), bf16[16,16,4096]{2,1,0:T(8,128)(2,1)}, u32[]{:S(2)}, u32[]{:S(2)}) async-start(bf16[16,16,4096]{2,1,0:T(8,128)(2,1)} %bitcast.255), calls=%async_computation.4 | async-start | bytes 4194304 | tf_op jit(solution)/shard_map/all_to_all | solution.py:170
  112.2 10.2 %all-to-all-start.1 = ((f32[16,1,512]{2,1,0:T(1,128)}), f32[16,1,512]{2,1,0:T(1,128)S(1)}, u32[]{:S(2)}, u32[]{:S(2)}) async-start(f32[16,1,512]{2,1,0:T(1,128)} %reshape.395), calls=%async_computation.1 | async-start | bytes 65536 | tf_op jit(solution)/shard_map/all_to_all | solution.py:177
  122.4 8.2 %copy-start.10 = (f32[16,1,512]{2,1,0:T(1,128)}, f32[16,1,512]{2,1,0:T(1,128)S(1)}, u32[]{:S(2)}) copy-start(f32[16,1,512]{2,1,0:T(1,128)S(1)} %all-to-all-done.1) | copy-start | bytes 98308
  122.4 46.2 %all-to-all-start.2 = ((f32[16,1,512]{2,1,0:T(1,128)}), f32[16,1,512]{2,1,0:T(1,128)}, u32[]{:S(2)}, u32[]{:S(2)}) async-start(f32[16,1,512]{2,1,0:T(1,128)} %reshape.397), calls=%async_computation.2 | async-start | bytes 65536 | tf_op jit(solution)/shard_map/all_to_all | solution.py:178
  165.3 19.5 %copy-start.2 = (bf16[4,2048,128]{2,1,0:T(8,128)(2,1)S(1)}, bf16[4,2048,128]{2,1,0:T(8,128)(2,1)}, u32[]{:S(2)}) copy-start(bf16[4,2048,128]{2,1,0:T(8,128)(2,1)} %get-tuple-element.85) | copy-start | bytes 6291460
  168.7 10.3 %all-to-all-start.5 = ((f32[16,1,512]{2,1,0:T(1,128)}), f32[16,1,512]{2,1,0:T(1,128)}, u32[]{:S(2)}, u32[]{:S(2)}) async-start(f32[16,1,512]{2,1,0:T(1,128)} %reshape.391), calls=%async_computation.5 | async-start | bytes 65536 | tf_op jit(solution)/shard_map/all_to_all | solution.py:177
  179.0 11.8 %all-to-all-start.6 = ((f32[16,1,512]{2,1,0:T(1,128)}), f32[16,1,512]{2,1,0:T(1,128)S(1)}, u32[]{:S(2)}, u32[]{:S(2)}) async-start(f32[16,1,512]{2,1,0:T(1,128)} %reshape.393), calls=%async_computation.6 | async-start | bytes 65536 | tf_op jit(solution)/shard_map/all_to_all | solution.py:178
  190.7 8.5 %copy-start.20 = (bf16[2,32,512]{2,1,0:T(8,128)(2,1)S(1)}, bf16[2,32,512]{2,1,0:T(8,128)(2,1)}, u32[]{:S(2)}) copy-start(bf16[2,32,512]{2,1,0:T(8,128)(2,1)} %param.19) | copy-start | bytes 196612
  190.7 8.5 %copy-start.22 = (s32[32]{0:T(128)S(1)}, s32[32]{0:T(128)}, u32[]{:S(2)}) copy-start(s32[32]{0:T(128)} %param.23) | copy-start | bytes 388
  191.4 53.5 %all-to-all-start.3 = ((bf16[16,16,4096]{2,1,0:T(8,128)(2,1)}), bf16[16,16,4096]{2,1,0:T(8,128)(2,1)S(1)}, u32[]{:S(2)}, u32[]{:S(2)}) async-start(bf16[16,16,4096]{2,1,0:T(8,128)(2,1)} %reshape.379), calls=%async_computation.3 | async-start | bytes 4194304 | tf_op jit(solution)/shard_map/all_to_all | solution.py:174
  199.3 7.4 %copy-start.21 = (bf16[2,32,4,128]{3,2,1,0:T(4,128)(2,1)}, bf16[2,32,4,128]{3,2,1,0:T(4,128)(2,1)S(1)}, u32[]{:S(2)}) copy-start(bf16[2,32,4,128]{3,2,1,0:T(4,128)(2,1)S(1)} %reshape.354) | copy-start | bytes 196612
  199.3 5.7 %copy-start.1 = (bf16[4,2048,128]{2,1,0:T(8,128)(2,1)S(1)}, bf16[4,2048,128]{2,1,0:T(8,128)(2,1)}, u32[]{:S(2)}) copy-start(bf16[4,2048,128]{2,1,0:T(8,128)(2,1)} %get-tuple-element.88) | copy-start | bytes 6291460
  244.8 62.4 %all-to-all-start.7 = ((bf16[16,16,4096]{2,1,0:T(8,128)(2,1)}), bf16[16,16,4096]{2,1,0:T(8,128)(2,1)}, u32[]{:S(2)}, u32[]{:S(2)}) async-start(bf16[16,16,4096]{2,1,0:T(8,128)(2,1)} %reshape.380), calls=%async_computation.7 | async-start | bytes 4194304 | tf_op jit(solution)/shard_map/all_to_all | solution.py:174
  249.7 9.3 %copy-start.11 = (f32[16,1,512]{2,1,0:T(1,128)S(1)}, f32[16,1,512]{2,1,0:T(1,128)}, u32[]{:S(2)}) copy-start(f32[16,1,512]{2,1,0:T(1,128)} %copy-done.10) | copy-start | bytes 98308
  300.7 2.5 copy-start.14
  303.2 3.3 %copy-start.7 = (f32[32,4,8,128]{3,2,1,0:T(8,128)S(1)}, f32[32,4,8,128]{3,2,1,0:T(8,128)}, u32[]{:S(2)}) copy-start(f32[32,4,8,128]{3,2,1,0:T(8,128)} %fusion.83) | copy-start | bytes 1572868
  303.2 3.3 %copy-start.16 = (f32[32,4,8]{2,1,0:T(4,128)S(1)}, f32[32,4,8]{2,1,0:T(4,128)}, u32[]{:S(2)}) copy-start(f32[32,4,8]{2,1,0:T(4,128)} %copy.228) | copy-start | bytes 12292
  303.2 3.3 %copy-start.17 = (f32[32,4,8]{2,1,0:T(4,128)S(1)}, f32[32,4,8]{2,1,0:T(4,128)}, u32[]{:S(2)}) copy-start(f32[32,4,8]{2,1,0:T(4,128)} %copy.238) | copy-start | bytes 12292
  307.2 3.4 %copy-start.15 = (f32[32,4,4,8]{0,3,2,1:T(8,128)S(1)}, f32[32,4,4,8]{0,3,2,1:T(8,128)}, u32[]{:S(2)}) copy-start(f32[32,4,4,8]{0,3,2,1:T(8,128)} %get-tuple-element.212) | copy-start | bytes 49156
  310.6 1.7 copy-start.4
  (7 other events, 8.7 us)
where the time goes:
time: 318 us; the launch traced here: 314 us
  waiting for transfers between devices  85.6 us (27%)
  matrix products  77.8 us (24%)
  local copies, waits for them, and re-layouts  75.7 us (24%)
  starting transfers between devices  45.4 us (14%)
  other arithmetic  28.5 us (9%)
    all_to_all x2, waiting for transfers between devices, per_device(): lax.all_to_all(sending, 'kv', split_axis=0, concat_axis=0, tiled=True)  51.5 us
    all_to_all x2, waiting for transfers between devices, per_device(): lax.all_to_all(results[0].astype(jnp.float32), 'kv', split_axis=0, concat...  34 us
    dot_general x8, matrix products, head_partial(): jnp.dot(weights, value_rows, preferred_element_type=jnp.float32)  27.4 us
    dot_general x8, matrix products, head_partial(): lax.dot_general(query_rows, key_rows, (((1,), (1,)), ((), ())), preferred...  18.4 us
    unnamed x62, local copies, waits for them, and re-layouts  16.3 us
    all_to_all x2, starting transfers between devices, per_device(): lax.all_to_all(results[2], 'kv', split_axis=0, concat_axis=0, tiled=True)  11.9 us
    convert_element_type x4, local copies, waits for them, and re-layouts, per_device(): results[0].astype(jnp.float32)  11.7 us
    all_to_all x2, starting transfers between devices, per_device(): lax.all_to_all(sending, 'kv', split_axis=0, concat_axis=0, tiled=True)  11.6 us
  transfers between devices with their start and end apart: 8, of which 4 were waited for; matrix products, arithmetic and copies ran while one was open for 54% of the time, Pallas kernels for 0%

commit v1 on v0

v1 whole, which is shorter than its diff:
```python
import functools
import math

import jax
import jax.numpy as jnp
from jax import lax
from jax.experimental import pallas as pl
from jax.experimental.pallas import tpu as pltpu
from jax.sharding import PartitionSpec as P

QUERY_HEADS = 32
KEY_VALUE_HEADS = 4
HEAD_SIZE = 128
SUFFIX_SLOTS = 32
DECODE_STEPS = 2
GROUP = QUERY_HEADS // KEY_VALUE_HEADS
WIDTH = QUERY_HEADS * HEAD_SIZE
LANES = 128

NEG = -1e30
SCALE = math.log2(math.e) / math.sqrt(HEAD_SIZE)
NT = (((1,), (1,)), ((), ()))
VMEM = 48 * 1024 * 1024


def head_columns(head):
    return slice(head * HEAD_SIZE, (head + 1) * HEAD_SIZE)


def stack_heads(query_rows, kv_head):
    return jnp.concatenate(
        [query_rows[:, head_columns(kv_head * GROUP + j)] for j in range(GROUP)], axis=0
    )


def values_and_ones(values):
    return jnp.concatenate([values, jnp.ones_like(values)], axis=1)


def attend_kernel(q_ref, k_ref, v_ref, out_ref):
    rows = q_ref.shape[0]
    lane = lax.broadcasted_iota(jnp.int32, (rows, LANES), 1)
    stats = jnp.zeros((rows, LANES), jnp.float32)
    for h in range(KEY_VALUE_HEADS):
        cols = head_columns(h)
        scores = lax.dot_general(
            stack_heads(q_ref, h), k_ref[:, cols], NT, preferred_element_type=jnp.float32
        )
        top = jnp.max(scores, axis=1, keepdims=True) * SCALE
        weights = jnp.exp2(scores * SCALE - top).astype(jnp.bfloat16)
        mixed = jnp.dot(
            weights, values_and_ones(v_ref[:, cols]), preferred_element_type=jnp.float32
        )
        total = mixed[:, HEAD_SIZE:]
        result = (mixed[:, :HEAD_SIZE] / total).astype(jnp.bfloat16)
        level = top + jnp.log2(total)
        for j in range(GROUP):
            head = h * GROUP + j
            part = slice(j * rows, (j + 1) * rows)
            out_ref[:, head_columns(head)] = result[part]
            stats = jnp.where(lane % QUERY_HEADS == head, level[part], stats)
    high = stats.astype(jnp.bfloat16).astype(jnp.float32)
    middle = (stats - high).astype(jnp.bfloat16).astype(jnp.float32)
    low = stats - high - middle
    packed = jnp.where(
        lane < QUERY_HEADS, high, jnp.where(lane < 2 * QUERY_HEADS, middle, low)
    )
    out_ref[:, WIDTH:] = packed.astype(jnp.bfloat16)


def attend(slots, keys, values, tile):
    count = slots.shape[0]
    tokens, width = keys.shape
    return pl.pallas_call(
        attend_kernel,
        grid=(count // tile,),
        in_specs=[
            pl.BlockSpec((tile, WIDTH), lambda i: (i, 0)),
            pl.BlockSpec((tokens, width), lambda i: (0, 0)),
            pl.BlockSpec((tokens, width), lambda i: (0, 0)),
        ],
        out_specs=pl.BlockSpec((tile, WIDTH + LANES), lambda i: (i, 0)),
        out_shape=jax.ShapeDtypeStruct((count, WIDTH + LANES), jnp.bfloat16),
        compiler_params=pltpu.CompilerParams(vmem_limit_bytes=VMEM),
        cost_estimate=pl.CostEstimate(
            flops=4 * count * WIDTH * tokens,
            bytes_accessed=4 * (count * WIDTH + tokens * width),
            transcendentals=count * QUERY_HEADS * tokens,
        ),
    )(slots, keys, values)


def own_kernel(q_ref, k_ref, v_ref, sk_ref, sv_ref, bias_ref, sbias_ref, out_ref, level_ref):
    rows = q_ref.shape[0]
    lane = lax.broadcasted_iota(jnp.int32, (rows, LANES), 1)
    levels = jnp.zeros((rows, LANES), jnp.float32)
    bias = jnp.concatenate([bias_ref[...]] * GROUP, axis=0)
    step_bias = jnp.concatenate([sbias_ref[...]] * GROUP, axis=0)
    for h in range(KEY_VALUE_HEADS):
        cols = head_columns(h)
        q = stack_heads(q_ref, h)
        first = lax.dot_general(q, k_ref[:, cols], NT, preferred_element_type=jnp.float32)
        second = lax.dot_general(q, sk_ref[:, cols], NT, preferred_element_type=jnp.float32)
        first = jnp.where(bias == 0, first * SCALE, NEG)
        second = jnp.where(step_bias == 0, second * SCALE, NEG)
        top = jnp.maximum(
            jnp.max(first, axis=1, keepdims=True), jnp.max(second, axis=1, keepdims=True)
        )
        mixed = jnp.dot(
            jnp.exp2(first - top).astype(jnp.bfloat16),
            values_and_ones(v_ref[:, cols]),
            preferred_element_type=jnp.float32,
        ) + jnp.dot(
            jnp.exp2(second - top).astype(jnp.bfloat16),
            values_and_ones(sv_ref[:, cols]),
            preferred_element_type=jnp.float32,
        )
        total = mixed[:, HEAD_SIZE:]
        result = mixed[:, :HEAD_SIZE] / total
        level = top + jnp.log2(total)
        for j in range(GROUP):
            head = h * GROUP + j
            part = slice(j * rows, (j + 1) * rows)
            out_ref[:, head_columns(head)] = result[part]
            levels = jnp.where(lane == head, level[part], levels)
    level_ref[...] = levels


def own_part(q, keys, values, step_keys, step_values, bias, step_bias):
    rows = q.shape[0]
    return pl.pallas_call(
        own_kernel,
        out_shape=(
            jax.ShapeDtypeStruct((rows, WIDTH), jnp.float32),
            jax.ShapeDtypeStruct((rows, LANES), jnp.float32),
        ),
        compiler_params=pltpu.CompilerParams(vmem_limit_bytes=VMEM),
        cost_estimate=pl.CostEstimate(
            flops=4 * rows * WIDTH * keys.shape[0],
            bytes_accessed=4 * keys.size,
            transcendentals=rows * QUERY_HEADS * keys.shape[0],
        ),
    )(q, keys, values, step_keys, step_values, bias, step_bias)


def merge_kernel(back_ref, place_ref, own_ref, level_ref, out_ref):
    packed = back_ref[:, WIDTH:].astype(jnp.float32).T
    path_level = (
        packed[:QUERY_HEADS]
        + packed[QUERY_HEADS : 2 * QUERY_HEADS]
        + packed[2 * QUERY_HEADS : 3 * QUERY_HEADS]
    )
    place = place_ref[...] > 0
    levels = level_ref[...]
    for head in range(QUERY_HEADS):
        cols = head_columns(head)
        own_level = levels[:, head : head + 1]
        level = jnp.where(place, path_level[head : head + 1, :], NEG)
        top = jnp.maximum(own_level, jnp.max(level, axis=1, keepdims=True))
        factor = jnp.exp2(level - top).astype(jnp.bfloat16)
        own_factor = jnp.exp2(own_level - top)
        numer = own_factor * own_ref[:, cols] + jnp.dot(
            factor, back_ref[:, cols], preferred_element_type=jnp.float32
        )
        denom = own_factor + jnp.sum(factor.astype(jnp.float32), axis=1, keepdims=True)
        out_ref[:, cols] = (numer / denom).astype(jnp.bfloat16)


def merge(back, place, own, level):
    return pl.pallas_call(
        merge_kernel,
        out_shape=jax.ShapeDtypeStruct(own.shape, jnp.bfloat16),
        compiler_params=pltpu.CompilerParams(vmem_limit_bytes=VMEM),
        cost_estimate=pl.CostEstimate(
            flops=2 * place.size * WIDTH, bytes_accessed=2 * back.size, transcendentals=0
        ),
    )(back, place, own, level)


def per_device(
    queries,
    shared_prefix_keys,
    shared_prefix_values,
    row_suffix_keys,
    row_suffix_values,
    step_keys,
    step_values,
    tree_blocks,
    block_slot,
    suffix_length,
):
    devices = lax.axis_size("kv")
    steps, rows, _ = queries.shape
    path = tree_blocks.shape[1]
    capacity = max(2, 2 * rows * path // devices)
    slots_all = devices * capacity
    blocks_flat = tree_blocks.reshape(-1)
    device_ids = jnp.arange(devices, dtype=jnp.int32)
    target = jnp.sum(
        jnp.where(blocks_flat[:, None] == device_ids[None, :], block_slot[None, :], 0), axis=1
    )
    entry = jnp.arange(rows * path, dtype=jnp.int32)
    rank = jnp.sum(
        (target[:, None] == target[None, :]) & (entry[None, :] < entry[:, None]),
        axis=1,
        dtype=jnp.int32,
    )
    slot_index = (target * capacity + rank).reshape(rows, path)
    place = jnp.sum(
        slot_index[:, :, None] == jnp.arange(slots_all, dtype=jnp.int32), axis=1
    ).astype(jnp.bfloat16)
    keys_flat = row_suffix_keys.reshape(rows * SUFFIX_SLOTS, -1)
    values_flat = row_suffix_values.reshape(rows * SUFFIX_SLOTS, -1)
    row_ids = jnp.arange(rows, dtype=jnp.int32)
    position = jnp.arange(rows * SUFFIX_SLOTS, dtype=jnp.int32)[None, :]
    bias = jnp.where(
        (position // SUFFIX_SLOTS == row_ids[:, None])
        & (position % SUFFIX_SLOTS < suffix_length[:, None]),
        0.0,
        NEG,
    )
    step_position = jnp.arange(steps * rows, dtype=jnp.int32)[None, :]
    latest_keys = step_keys.reshape(steps * rows, -1)
    latest_values = step_values.reshape(steps * rows, -1)
    tile = math.gcd(64, slots_all)
    exchange = functools.partial(
        lax.all_to_all, axis_name="kv", split_axis=0, concat_axis=0, tiled=True
    )
    received, owns, backs = [], [], []
    for t in range(steps):
        sending = lax.dot_general(
            place, queries[t], (((0,), (0,)), ((), ())), preferred_element_type=jnp.float32
        ).astype(jnp.bfloat16)
        received.append(exchange(sending.reshape(devices, capacity, WIDTH)))
    for t in range(steps):
        step_bias = jnp.where(
            (step_position % rows == row_ids[:, None]) & (step_position // rows <= t), 0.0, NEG
        )
        owns.append(
            own_part(
                queries[t], keys_flat, values_flat, latest_keys, latest_values, bias, step_bias
            )
        )
    for t in range(steps):
        result = attend(
            received[t].reshape(slots_all, WIDTH), shared_prefix_keys, shared_prefix_values, tile
        )
        backs.append(exchange(result.reshape(devices, capacity, WIDTH + LANES)))
    return jnp.stack(
        [
            merge(backs[t].reshape(slots_all, WIDTH + LANES), place, *owns[t])
            for t in range(steps)
        ]
    )


def solution(mesh):
    return jax.shard_map(
        per_device,
        mesh=mesh,
        in_specs=(
            P(None, ("groups", "kv"), None),
            P("kv", None),
            P("kv", None),
            P(("groups", "kv"), None, None),
            P(("groups", "kv"), None, None),
            P(None, ("groups", "kv"), None),
            P(None, ("groups", "kv"), None),
            P(("groups", "kv"), None),
            P(),
            P(("groups", "kv")),
        ),
        out_specs=P(None, ("groups", "kv"), None),
        check_vma=False,
    )
```

time: 318 us -> 233 us (0.73)
  matrix products: 77.8 us -> 5.06 us
  local copies, waits for them, and re-layouts: 75.7 us -> 12.4 us
  waiting for transfers between devices: 85.6 us -> 141 us
  Pallas kernels: 0 us -> 49.6 us
  other arithmetic: 28.5 us -> 1.98 us
  starting transfers between devices: 45.4 us -> 21.6 us
    dot_general x32 -> x2, matrix products: 77.8 us -> 5.06 us  [per_device(): lax.dot_general(place, queries[t], (((0,), (0,)), ((), ())), preferred_el...]
    all_to_all x8 -> x4, waiting for transfers between devices: 85.6 us -> 141 us  [the longest x2 76 us: per_device(): received.append(exchange(sending.reshape(devices, capacity, WIDTH)))]
    pallas_call x0 -> x6, Pallas kernels: none -> 49.6 us  [the longest x2 27.8 us: attend(): pl.pallas_call(attend_kernel, grid=(count // tile,), in_specs=[pl.BlockSp...]
    all_to_all x8 -> x4, starting transfers between devices: 45.4 us -> 21.6 us  [the longest x2 11.6 us: per_device(): received.append(exchange(sending.reshape(devices, capacity, WIDTH)))]
    reduce_sum x12 -> x2, other arithmetic: 16.2 us -> 0.27 us  [the longest x1 0.17 us: per_device(): jnp.sum((target[:, None] == target[None, :]) & (entry[None, :] < entry[:,...]
    convert_element_type x6 -> x0, local copies, waits for them, and re-layouts: 12 us -> none  [the longest x4 11.7 us: per_device(): results[0].astype(jnp.float32)]
    dot_general x6 -> x0, local copies, waits for them, and re-layouts: 9.66 us -> none  [the longest x2 5.77 us: per_device(): jnp.dot(placing, mixed_back.reshape(slots_all, QUERY_HEADS * HEAD_SIZE),...]
    reshape x16 -> x0, local copies, waits for them, and re-layouts: 9.07 us -> none  [the longest x2 3.41 us: attend_block(): tile_list.reshape(row_count, KEY_VALUE_HEADS, head_group, HEAD_SIZE)]
  transfers between devices with their start and end apart: 8 -> 4, of which waited for: 4 -> 4; matrix products, arithmetic and copies ran while one was open for 54% -> 1% of each run, Pallas kernels for 0% -> 17%
where the time goes in v1:
time: 233 us; the launch traced here: 232 us
  waiting for transfers between devices  141 us (61%)
  Pallas kernels  49.6 us (21%)
  starting transfers between devices  21.6 us (9%)
  local copies, waits for them, and re-layouts  12.4 us (5%)
  matrix products  5.06 us (2%)
    all_to_all x2, waiting for transfers between devices, per_device(): received.append(exchange(sending.reshape(devices, capacity, WIDTH)))  76 us
    all_to_all x2, waiting for transfers between devices, per_device(): backs.append(exchange(result.reshape(devices, capacity, WIDTH + LANES)))  65.2 us
    pallas_call x2, Pallas kernels, attend(): pl.pallas_call(attend_kernel, grid=(count // tile,), in_specs=[pl.BlockSp...  27.8 us
    pallas_call x2, Pallas kernels, merge(): pl.pallas_call(merge_kernel, out_shape=jax.ShapeDtypeStruct(own.shape, jn...  16.8 us
    all_to_all x2, starting transfers between devices, per_device(): received.append(exchange(sending.reshape(devices, capacity, WIDTH)))  11.6 us
    unnamed x31, local copies, waits for them, and re-layouts  11.1 us
    all_to_all x2, starting transfers between devices, per_device(): backs.append(exchange(result.reshape(devices, capacity, WIDTH + LANES)))  9.96 us
    dot_general x2, matrix products, per_device(): lax.dot_general(place, queries[t], (((0,), (0,)), ((), ())), preferred_el...  5.06 us
  transfers between devices with their start and end apart: 4, of which 4 were waited for; matrix products, arithmetic and copies ran while one was open for 1% of the time, Pallas kernels for 17%

profile of v1, /device:TPU:11, one launch (start us, length us, event | category | flops | bytes accessed | tf_op | source)
XLA Modules:
  0.0 232.0 jit_solution(9109160226720866858)
XLA Ops:
  2.1 3.0 %convolution_convert_fusion = bf16[256,4096]{1,0:T(8,128)(2,1)} fusion(bf16[32,256]{1,0:T(8,128)(2,1)S(1)} %convert_element_type.17.place_ref, bf16[2,32,4096]{2,1,0:T(8,128)(2,1)} %param.10), kind=kOutput, calls=%fused_computation | convolution fusion | flops 68157440 | bytes 2375680 | tf_op jit(solution)/shard_map/dot_general | solution.py:231
  5.1 6.7 %all-to-all-start.2 = ((bf16[16,16,4096]{2,1,0:T(8,128)(2,1)}), bf16[16,16,4096]{2,1,0:T(8,128)(2,1)S(1)}, u32[]{:S(2)}, u32[]{:S(2)}) async-start(bf16[16,16,4096]{2,1,0:T(8,128)(2,1)} %bitcast.36), calls=%async_computation.2 | async-start | bytes 4194304 | tf_op jit(solution)/shard_map/all_to_all | solution.py:234
  11.8 2.0 convolution_convert_fusion.1
  13.9 45.4 %all-to-all-done.2 = bf16[16,16,4096]{2,1,0:T(8,128)(2,1)S(1)} async-done(((bf16[16,16,4096]{2,1,0:T(8,128)(2,1)}), bf16[16,16,4096]{2,1,0:T(8,128)(2,1)S(1)}, u32[]{:S(2)}, u32[]{:S(2)}) %all-to-all-start.2) | async-done | bytes 2097184 | tf_op jit(solution)/shard_map/all_to_all | solution.py:234
  59.2 1.3 copy-done.4
  60.6 4.9 %all-to-all-start = ((bf16[16,16,4096]{2,1,0:T(8,128)(2,1)}), bf16[16,16,4096]{2,1,0:T(8,128)(2,1)S(1)}, u32[]{:S(2)}, u32[]{:S(2)}) async-start(bf16[16,16,4096]{2,1,0:T(8,128)(2,1)} %bitcast.35), calls=%async_computation | async-start | bytes 4194304 | tf_op jit(solution)/shard_map/all_to_all | solution.py:234
  65.5 1.6 copy-done.5
  67.1 1.2 copy-done.11
  68.3 13.9 %shard_map.103 = bf16[256,4224]{1,0:T(8,128)(2,1)} custom-call(bf16[256,4096]{1,0:T(8,128)(2,1)S(1)} %bitcast.28, bf16[1024,512]{1,0:T(8,128)(2,1)S(1)} %copy-done.10, bf16[1024,512]{1,0:T(8,128)(2,1)S(1)} %copy-done.11), custom_call_target="tpu_custom_call" | custom-call | flops 4294967296 | bytes 6291456 | tf_op jit(solution)/shard_map/pallas_call | solution.py:74
  82.2 30.7 %all-to-all-done = bf16[16,16,4096]{2,1,0:T(8,128)(2,1)S(1)} async-done(((bf16[16,16,4096]{2,1,0:T(8,128)(2,1)}), bf16[16,16,4096]{2,1,0:T(8,128)(2,1)S(1)}, u32[]{:S(2)}, u32[]{:S(2)}) %all-to-all-start) | async-done | bytes 2097184 | tf_op jit(solution)/shard_map/all_to_all | solution.py:234
  112.9 1.3 copy-done.2
  114.2 4.9 %all-to-all-start.3 = ((bf16[16,16,4224]{2,1,0:T(8,128)(2,1)}), bf16[16,16,4224]{2,1,0:T(8,128)(2,1)S(1)}, u32[]{:S(2)}, u32[]{:S(2)}) async-start(bf16[16,16,4224]{2,1,0:T(8,128)(2,1)} %bitcast.38), calls=%async_computation.3 | async-start | bytes 4325376 | tf_op jit(solution)/shard_map/all_to_all | solution.py:248
  119.1 1.6 copy-done.3
  120.7 1.2 copy-done.12
  121.9 13.9 %shard_map.100 = bf16[256,4224]{1,0:T(8,128)(2,1)} custom-call(bf16[256,4096]{1,0:T(8,128)(2,1)S(1)} %bitcast.27, bf16[1024,512]{1,0:T(8,128)(2,1)S(1)} %copy-done.10, bf16[1024,512]{1,0:T(8,128)(2,1)S(1)} %copy-done.12), custom_call_target="tpu_custom_call" | custom-call | flops 4294967296 | bytes 6291456 | tf_op jit(solution)/shard_map/pallas_call | solution.py:74
  135.8 32.1 %all-to-all-done.3 = bf16[16,16,4224]{2,1,0:T(8,128)(2,1)S(1)} async-done(((bf16[16,16,4224]{2,1,0:T(8,128)(2,1)}), bf16[16,16,4224]{2,1,0:T(8,128)(2,1)S(1)}, u32[]{:S(2)}, u32[]{:S(2)}) %all-to-all-start.3) | async-done | bytes 2162720 | tf_op jit(solution)/shard_map/all_to_all | solution.py:248
  168.0 5.1 %all-to-all-start.1 = ((bf16[16,16,4224]{2,1,0:T(8,128)(2,1)}), bf16[16,16,4224]{2,1,0:T(8,128)(2,1)}, u32[]{:S(2)}, u32[]{:S(2)}) async-start(bf16[16,16,4224]{2,1,0:T(8,128)(2,1)} %bitcast.37), calls=%async_computation.1 | async-start | bytes 4325376 | tf_op jit(solution)/shard_map/all_to_all | solution.py:248
  173.2 1.1 slice_bitcast_fusion.1
  174.3 1.2 copy-done.1
  175.5 2.5 %shard_map.104 = (f32[32,4096]{1,0:T(8,128)S(1)}, f32[32,128]{1,0:T(8,128)S(1)}) custom-call(bf16[32,4096]{1,0:T(8,128)(2,1)S(1)} %get-tuple-element.14.q_ref, bf16[1024,512]{1,0:T(8,128)(2,1)S(1)} %bitcast.23, bf16[1024,512]{1,0:T(8,128)(2,1)S(1)} %bitcast.25, bf16[64,512]{1,0:T(8,128)(2,1)S(1)} %bitcast.31, bf16[64,512]{1,0:T(8,128)(2,1)S(1)} %bitcast.33, ...), custom_call_target="tpu_custom_call" | custom-call | flops 536870912 | bytes 2097152 | tf_op jit(solution)/shard_map/pallas_call | solution.py:131
  178.0 2.5 %shard_map.101 = (f32[32,4096]{1,0:T(8,128)S(1)}, f32[32,128]{1,0:T(8,128)S(1)}) custom-call(bf16[32,4096]{1,0:T(8,128)(2,1)S(1)} %get-tuple-element.13.q_ref, bf16[1024,512]{1,0:T(8,128)(2,1)S(1)} %bitcast.24, bf16[1024,512]{1,0:T(8,128)(2,1)S(1)} %bitcast.26, bf16[64,512]{1,0:T(8,128)(2,1)S(1)} %bitcast.32, bf16[64,512]{1,0:T(8,128)(2,1)S(1)} %bitcast.34, ...), custom_call_target="tpu_custom_call" | custom-call | flops 536870912 | bytes 2097152 | tf_op jit(solution)/shard_map/pallas_call | solution.py:131
  181.2 7.6 %shard_map.105 = bf16[32,4096]{1,0:T(8,128)(2,1)S(1)} custom-call(bf16[256,4224]{1,0:T(8,128)(2,1)S(1)} %bitcast.22, bf16[32,256]{1,0:T(8,128)(2,1)S(1)} %convert_element_type.17.place_ref, f32[32,4096]{1,0:T(8,128)S(1)} %get-tuple-element.11.own_ref, f32[32,128]{1,0:T(8,128)S(1)} %get-tuple-element.12.level_ref), custom_call_target="tpu_custom_call" | custom-call | flops 67108864 | bytes 2162688 | tf_op jit(solution)/shard_map/pallas_call | solution.py:170
  188.8 33.1 %all-to-all-done.1 = bf16[16,16,4224]{2,1,0:T(8,128)(2,1)} async-done(((bf16[16,16,4224]{2,1,0:T(8,128)(2,1)}), bf16[16,16,4224]{2,1,0:T(8,128)(2,1)}, u32[]{:S(2)}, u32[]{:S(2)}) %all-to-all-start.1) | async-done | bytes 2162720 | tf_op jit(solution)/shard_map/all_to_all | solution.py:248
  221.9 9.2 %shard_map.102 = bf16[32,4096]{1,0:T(8,128)(2,1)S(1)} custom-call(bf16[256,4224]{1,0:T(8,128)(2,1)} %bitcast.4.back_ref, bf16[32,256]{1,0:T(8,128)(2,1)S(1)} %convert_element_type.17.place_ref, f32[32,4096]{1,0:T(8,128)S(1)} %copy-done.7, f32[32,128]{1,0:T(8,128)S(1)} %get-tuple-element.10.level_ref), custom_call_target="tpu_custom_call" | custom-call | flops 67108864 | bytes 2162688 | tf_op jit(solution)/shard_map/pallas_call | solution.py:170
  (38 shorter events, 3.8 us)
Async XLA Ops:
  5.1 6.7 %copy-start.13 = (bf16[2,32,4096]{2,1,0:T(8,128)(2,1)S(1)}, bf16[2,32,4096]{2,1,0:T(8,128)(2,1)}, u32[]{:S(2)}) copy-start(bf16[2,32,4096]{2,1,0:T(8,128)(2,1)} %param.10) | copy-start | bytes 1572868
  5.1 54.1 %all-to-all-start.2 = ((bf16[16,16,4096]{2,1,0:T(8,128)(2,1)}), bf16[16,16,4096]{2,1,0:T(8,128)(2,1)S(1)}, u32[]{:S(2)}, u32[]{:S(2)}) async-start(bf16[16,16,4096]{2,1,0:T(8,128)(2,1)} %bitcast.36), calls=%async_computation.2 | async-start | bytes 4194304 | tf_op jit(solution)/shard_map/all_to_all | solution.py:234
  13.9 51.6 %copy-start.10 = (bf16[1024,512]{1,0:T(8,128)(2,1)S(1)}, bf16[1024,512]{1,0:T(8,128)(2,1)}, u32[]{:S(2)}) copy-start(bf16[1024,512]{1,0:T(8,128)(2,1)} %k_ref.3) | copy-start | bytes 3145732
  59.2 1.3 copy-start.4
  60.6 52.3 %all-to-all-start = ((bf16[16,16,4096]{2,1,0:T(8,128)(2,1)}), bf16[16,16,4096]{2,1,0:T(8,128)(2,1)S(1)}, u32[]{:S(2)}, u32[]{:S(2)}) async-start(bf16[16,16,4096]{2,1,0:T(8,128)(2,1)} %bitcast.35), calls=%async_computation | async-start | bytes 4194304 | tf_op jit(solution)/shard_map/all_to_all | solution.py:234
  65.5 1.6 copy-start.5
  67.1 1.2 copy-start.11
  112.9 1.3 copy-start.2
  114.2 53.7 %all-to-all-start.3 = ((bf16[16,16,4224]{2,1,0:T(8,128)(2,1)}), bf16[16,16,4224]{2,1,0:T(8,128)(2,1)S(1)}, u32[]{:S(2)}, u32[]{:S(2)}) async-start(bf16[16,16,4224]{2,1,0:T(8,128)(2,1)} %bitcast.38), calls=%async_computation.3 | async-start | bytes 4325376 | tf_op jit(solution)/shard_map/all_to_all | solution.py:248
  119.1 1.6 copy-start.3
  120.7 1.2 copy-start.12
  167.9 5.1 %copy-start.14 = (s32[32]{0:T(128)S(1)}, s32[32]{0:T(128)}, u32[]{:S(2)}) copy-start(s32[32]{0:T(128)} %param.19) | copy-start | bytes 388
  167.9 6.3 %copy-start = (bf16[32,32,512]{2,1,0:T(8,128)(2,1)S(1)}, bf16[32,32,512]{2,1,0:T(8,128)(2,1)}, u32[]{:S(2)}) copy-start(bf16[32,32,512]{2,1,0:T(8,128)(2,1)} %param.13) | copy-start | bytes 3145732
  167.9 6.3 %copy-start.8 = (bf16[2,32,512]{2,1,0:T(8,128)(2,1)S(1)}, bf16[2,32,512]{2,1,0:T(8,128)(2,1)}, u32[]{:S(2)}) copy-start(bf16[2,32,512]{2,1,0:T(8,128)(2,1)} %param.15) | copy-start | bytes 196612
  168.0 6.3 %copy-start.9 = (bf16[2,32,512]{2,1,0:T(8,128)(2,1)S(1)}, bf16[2,32,512]{2,1,0:T(8,128)(2,1)}, u32[]{:S(2)}) copy-start(bf16[2,32,512]{2,1,0:T(8,128)(2,1)} %param.16) | copy-start | bytes 196612
  168.0 54.0 %all-to-all-start.1 = ((bf16[16,16,4224]{2,1,0:T(8,128)(2,1)}), bf16[16,16,4224]{2,1,0:T(8,128)(2,1)}, u32[]{:S(2)}, u32[]{:S(2)}) async-start(bf16[16,16,4224]{2,1,0:T(8,128)(2,1)} %bitcast.37), calls=%async_computation.1 | async-start | bytes 4325376 | tf_op jit(solution)/shard_map/all_to_all | solution.py:248
  174.3 1.2 copy-start.1
  180.4 0.8 copy-start.6
  181.2 40.7 %copy-start.7 = (f32[32,4096]{1,0:T(8,128)S(1)}, f32[32,4096]{1,0:T(8,128)}, u32[]{:S(2)}) copy-start(f32[32,4096]{1,0:T(8,128)} %copy-done.6) | copy-start | bytes 1572868

commit v2 on v1

--- a/solution.py
+++ b/solution.py
@@ -175,6 +175,23 @@
             flops=2 * place.size * WIDTH, bytes_accessed=2 * back.size, transcendentals=0
         ),
     )(back, place, own, level)
+
+
+def exchange_masks(devices, turn):
+    masks = [1 << b for b in reversed(range((devices - 1).bit_length()))]
+    if turn % 2 and 2 in masks:
+        masks.remove(2)
+        masks.insert(0, 2)
+    return masks
+
+
+def gather_rows(block, devices, masks):
+    order, held = [0], block
+    for mask in masks:
+        partner = lax.ppermute(held, "kv", [(i, i ^ mask) for i in range(devices)])
+        held = jnp.concatenate([held, partner], axis=0)
+        order = order + [o ^ mask for o in order]
+    return order, held
 
 
 def per_device(
@@ -227,11 +244,31 @@
         lax.all_to_all, axis_name="kv", split_axis=0, concat_axis=0, tiled=True
     )
     received, owns, backs = [], [], []
-    for t in range(steps):
-        sending = lax.dot_general(
-            place, queries[t], (((0,), (0,)), ((), ())), preferred_element_type=jnp.float32
-        ).astype(jnp.bfloat16)
-        received.append(exchange(sending.reshape(devices, capacity, WIDTH)))
+    if 4 * capacity >= rows and devices & (devices - 1) == 0:
+        me = lax.axis_index("kv")
+        everyone = lax.all_gather(slot_index, "kv", axis=0)
+        wanted = me * capacity + jnp.arange(capacity, dtype=jnp.int32)
+        filled = jnp.any(everyone[:, None, :, :] == wanted[None, :, None, None], axis=3)
+        for t in range(steps):
+            order, gathered = gather_rows(queries[t], devices, exchange_masks(devices, t))
+            sender = jnp.asarray(order, jnp.int32) ^ me
+            chosen = (
+                filled[:, :, None, :] & (device_ids[:, None] == sender[None, :])[:, None, :, None]
+            ).astype(jnp.bfloat16)
+            received.append(
+                jnp.dot(
+                    chosen.reshape(slots_all, devices * rows),
+                    gathered,
+                    preferred_element_type=jnp.float32,
+                ).astype(jnp.bfloat16)
+            )
+    else:
+        for t in range(steps):
+            sending = lax.dot_general(
+                place, queries[t], (((0,), (0,)), ((), ())), preferred_element_type=jnp.float32
+            ).astype(jnp.bfloat16)
+            tiles = exchange(sending.reshape(devices, capacity, WIDTH))
+            received.append(tiles.reshape(slots_all, WIDTH))
     for t in range(steps):
         step_bias = jnp.where(
             (step_position % rows == row_ids[:, None]) & (step_position // rows <= t), 0.0, NEG
@@ -243,7 +280,7 @@
         )
     for t in range(steps):
         result = attend(
-            received[t].reshape(slots_all, WIDTH), shared_prefix_keys, shared_prefix_values, tile
+            received[t], shared_prefix_keys, shared_prefix_values, tile
         )
         backs.append(exchange(result.reshape(devices, capacity, WIDTH + LANES)))
     return jnp.stack(

time: 233 us -> 237 us (1.017)
  waiting for transfers between devices: 141 us -> 84.8 us
  blocking collectives: 0 us -> 37 us
  local copies, waits for them, and re-layouts: 12.4 us -> 24.7 us
  other arithmetic: 1.98 us -> 11.8 us
    all_to_all x2 -> x0, waiting for transfers between devices: 76 us -> none  [per_device(): received.append(exchange(sending.reshape(devices, capacity, WIDTH)))]
    all_gather x0 -> x1, blocking collectives: none -> 37 us  [per_device(): everyone = lax.all_gather(slot_index, 'kv', axis=0)]
    ppermute x0 -> x8, waiting for transfers between devices: none -> 32.8 us  [gather_rows(): partner = lax.ppermute(held, 'kv', [(i, i ^ mask) for i in range(devices)])]
    all_to_all x2, waiting for transfers between devices: 65.2 us -> 51.9 us  [per_device(): backs.append(exchange(result.reshape(devices, capacity, WIDTH + LANES)))]
    all_to_all x2 -> x0, starting transfers between devices: 11.6 us -> none  [per_device(): received.append(exchange(sending.reshape(devices, capacity, WIDTH)))]
    ppermute x0 -> x8, starting transfers between devices: none -> 10.3 us  [gather_rows(): partner = lax.ppermute(held, 'kv', [(i, i ^ mask) for i in range(devices)])]
    concatenate x0 -> x6, other arithmetic: none -> 7.4 us  [gather_rows(): held = jnp.concatenate([held, partner], axis=0)]
    concatenate x0 -> x2, local copies, waits for them, and re-layouts: none -> 6.28 us  [gather_rows(): held = jnp.concatenate([held, partner], axis=0)]
  transfers between devices with their start and end apart: 4 -> 10, of which waited for: 4 -> 5; matrix products, arithmetic and copies ran while one was open for 1% -> 17% of each run, Pallas kernels for 17% -> 17%
where the time goes in v2:
time: 237 us; the launch traced here: 236 us
  waiting for transfers between devices  84.8 us (36%)
  Pallas kernels  49.6 us (21%)
  blocking collectives  37 us (16%)
  local copies, waits for them, and re-layouts  24.7 us (10%)
  starting transfers between devices  20.7 us (9%)
  other arithmetic  11.8 us (5%)
  matrix products  7.18 us (3%)
    all_to_all x2, waiting for transfers between devices, per_device(): backs.append(exchange(result.reshape(devices, capacity, WIDTH + LANES)))  51.9 us
    all_gather x1, blocking collectives, per_device(): everyone = lax.all_gather(slot_index, 'kv', axis=0)  37 us
    ppermute x8, waiting for transfers between devices, gather_rows(): partner = lax.ppermute(held, 'kv', [(i, i ^ mask) for i in range(devices)])  32.8 us
    pallas_call x2, Pallas kernels, attend(): pl.pallas_call(attend_kernel, grid=(count // tile,), in_specs=[pl.BlockSp...  27.9 us
    pallas_call x2, Pallas kernels, merge(): pl.pallas_call(merge_kernel, out_shape=jax.ShapeDtypeStruct(own.shape, jn...  16.8 us
    unnamed x30, local copies, waits for them, and re-layouts  11.6 us
    all_to_all x2, starting transfers between devices, per_device(): backs.append(exchange(result.reshape(devices, capacity, WIDTH + LANES)))  10.5 us
    ppermute x8, starting transfers between devices, gather_rows(): partner = lax.ppermute(held, 'kv', [(i, i ^ mask) for i in range(devices)])  10.3 us
  transfers between devices with their start and end apart: 10, of which 5 were waited for; matrix products, arithmetic and copies ran while one was open for 17% of the time, Pallas kernels for 17%

profile of v2, /device:TPU:11, one launch (start us, length us, event | category | flops | bytes accessed | tf_op | source)
XLA Modules:
  0.0 236.0 jit_solution(15615965547061331951)
XLA Ops:
  1.4 2.3 collective-permute-start
  8.3 2.4 %collective-permute-start.5 = (bf16[64,4096]{1,0:T(8,128)(2,1)S(1)}, bf16[64,4096]{1,0:T(8,128)(2,1)S(1)}, u32[]{:S(2)}, u32[]{:S(2)}) collective-permute-start(bf16[64,4096]{1,0:T(8,128)(2,1)S(1)} %pad_maximum_fusion.5), channel_id=1, source_target_pairs={{0,8},{1,9},{2,10},{3,11},{4,12},{5,13},{6,14},{7,15},{8,0},{9,1},... | collective-permute-start | bytes 1572872 | tf_op jit(solution)/shard_map/ppermute | solution.py:191
  11.6 26.1 %collective-permute-done.5 = bf16[64,4096]{1,0:T(8,128)(2,1)S(1)} collective-permute-done((bf16[64,4096]{1,0:T(8,128)(2,1)S(1)}, bf16[64,4096]{1,0:T(8,128)(2,1)S(1)}, u32[]{:S(2)}, u32[]{:S(2)}) %collective-permute-start.5) | collective-permute-done | bytes 524320 | tf_op jit(solution)/shard_map/ppermute | solution.py:191
  39.0 37.0 %all_gather.3 = s32[16,32,4]{1,2,0:T(4,128)S(1)} all-gather(s32[1,32,4]{1,2,0:T(4,128)S(1)} %copy.19), channel_id=1, replica_groups=mesh['groups'=2,'kv'=16] {'kv'}, dimensions={0}, use_global_device_ids=true | all-gather | bytes 8704 | tf_op jit(solution)/shard_map/all_gather | solution.py:249
  77.1 3.0 %collective-permute-start.1 = (bf16[64,4096]{1,0:T(8,128)(2,1)}, bf16[64,4096]{1,0:T(8,128)(2,1)S(1)}, u32[]{:S(2)}, u32[]{:S(2)}) collective-permute-start(bf16[64,4096]{1,0:T(8,128)(2,1)} %pad_maximum_fusion.4), channel_id=1, source_target_pairs={{0,4},{1,5},{2,6},{3,7},{4,0},{5,1},{6,2},{7,3},{8,12},{9,13},{10,... | collective-permute-start | bytes 1572872 | tf_op jit(solution)/shard_map/ppermute | solution.py:191
  83.5 2.6 %and.137 = pred[256,512]{1,0:T(32,128)(4,1)} reshape(pred[16,16,16,32]{3,2,1,0:T(8,128)(4,1)} %get-tuple-element.18) | data formatting | bytes 262144 | tf_op jit(solution)/shard_map/and | solution.py:256
  86.9 5.6 %collective-permute-done.1 = bf16[64,4096]{1,0:T(8,128)(2,1)S(1)} collective-permute-done((bf16[64,4096]{1,0:T(8,128)(2,1)}, bf16[64,4096]{1,0:T(8,128)(2,1)S(1)}, u32[]{:S(2)}, u32[]{:S(2)}) %collective-permute-start.1) | collective-permute-done | bytes 524320 | tf_op jit(solution)/shard_map/ppermute | solution.py:191
  97.0 3.2 %constant_dynamic-update-slice_fusion.5 = bf16[512,4096]{1,0:T(8,128)(2,1)} fusion(bf16[512,4096]{1,0:T(8,128)(2,1)} %constant_dynamic-update-slice_fusion.6, bf16[256,4096]{1,0:T(8,128)(2,1)} %collective-permute-done.7), kind=kLoop, calls=%fused_computation.27 | loop fusion | bytes 4194304 | tf_op jit(solution)/shard_map/concatenate | solution.py:192
  100.1 3.6 %convolution_convert_fusion.q_ref = bf16[256,4096]{1,0:T(8,128)(2,1)S(1)} fusion(pred[256,512]{1,0:T(32,128)(4,1)S(1)} %copy-done.8, bf16[512,4096]{1,0:T(8,128)(2,1)} %constant_dynamic-update-slice_fusion.5), kind=kOutput, calls=%fused_computation | convolution fusion | flops 1074790400 | bytes 6422528 | tf_op jit(solution)/shard_map/dot_general | solution.py:259
  103.7 14.0 %shard_map.121 = bf16[256,4224]{1,0:T(8,128)(2,1)} custom-call(bf16[256,4096]{1,0:T(8,128)(2,1)S(1)} %convolution_convert_fusion.q_ref, bf16[1024,512]{1,0:T(8,128)(2,1)S(1)} %copy-done.4, bf16[1024,512]{1,0:T(8,128)(2,1)S(1)} %copy-done.6), custom_call_target="tpu_custom_call" | custom-call | flops 4294967296 | bytes 6291456 | tf_op jit(solution)/shard_map/pallas_call | solution.py:74
  117.7 5.6 %all-to-all-start.1 = ((bf16[16,16,4224]{2,1,0:T(8,128)(2,1)}), bf16[16,16,4224]{2,1,0:T(8,128)(2,1)S(1)}, u32[]{:S(2)}, u32[]{:S(2)}) async-start(bf16[16,16,4224]{2,1,0:T(8,128)(2,1)} %bitcast.38), calls=%async_computation.1 | async-start | bytes 4325376 | tf_op jit(solution)/shard_map/all_to_all | solution.py:285
  123.3 2.8 %pad_maximum_fusion = bf16[256,4096]{1,0:T(8,128)(2,1)} fusion(bf16[128,4096]{1,0:T(8,128)(2,1)} %collective-permute-done.2, bf16[64,4096]{1,0:T(8,128)(2,1)S(1)} %collective-permute-done.1, bf16[32,4096]{1,0:T(8,128)(2,1)S(1)} %collective-permute-done, bf16[32,4096]{1,0:T(8,128)(2,1)S(1)} %get-tuple-element.13.q_ref), kind=kLoop, calls=%fused_computation.2 | loop fusion | flops 8388608 | bytes 4194304 | tf_op jit(solution)/shard_map/concatenate | solution.py:192
  126.4 2.7 %and.127 = pred[256,512]{1,0:T(32,128)(4,1)} reshape(pred[16,16,16,32]{3,2,1,0:T(8,128)(4,1)} %get-tuple-element.17) | data formatting | bytes 262144 | tf_op jit(solution)/shard_map/and | solution.py:256
  130.6 2.3 constant_dynamic-update-slice_fusion.1
  132.9 3.1 %constant_dynamic-update-slice_fusion = bf16[512,4096]{1,0:T(8,128)(2,1)} fusion(bf16[512,4096]{1,0:T(8,128)(2,1)} %constant_dynamic-update-slice_fusion.1, bf16[256,4096]{1,0:T(8,128)(2,1)} %collective-permute-done.3), kind=kLoop, calls=%fused_computation.22 | loop fusion | bytes 4194304 | tf_op jit(solution)/shard_map/concatenate | solution.py:192
  136.1 3.6 %convolution_convert_fusion.1.q_ref = bf16[256,4096]{1,0:T(8,128)(2,1)S(1)} fusion(pred[256,512]{1,0:T(32,128)(4,1)S(1)} %copy-done.9, bf16[512,4096]{1,0:T(8,128)(2,1)} %constant_dynamic-update-slice_fusion), kind=kOutput, calls=%fused_computation.1 | convolution fusion | flops 1074790400 | bytes 6422528 | tf_op jit(solution)/shard_map/dot_general | solution.py:259
  139.7 14.0 %shard_map.118 = bf16[256,4224]{1,0:T(8,128)(2,1)} custom-call(bf16[256,4096]{1,0:T(8,128)(2,1)S(1)} %convolution_convert_fusion.1.q_ref, bf16[1024,512]{1,0:T(8,128)(2,1)S(1)} %copy-done.5, bf16[1024,512]{1,0:T(8,128)(2,1)S(1)} %copy-done.7), custom_call_target="tpu_custom_call" | custom-call | flops 4294967296 | bytes 6291456 | tf_op jit(solution)/shard_map/pallas_call | solution.py:74
  153.6 18.5 %all-to-all-done.1 = bf16[16,16,4224]{2,1,0:T(8,128)(2,1)S(1)} async-done(((bf16[16,16,4224]{2,1,0:T(8,128)(2,1)}), bf16[16,16,4224]{2,1,0:T(8,128)(2,1)S(1)}, u32[]{:S(2)}, u32[]{:S(2)}) %all-to-all-start.1) | async-done | bytes 2162720 | tf_op jit(solution)/shard_map/all_to_all | solution.py:285
  172.1 4.9 %all-to-all-start = ((bf16[16,16,4224]{2,1,0:T(8,128)(2,1)}), bf16[16,16,4224]{2,1,0:T(8,128)(2,1)}, u32[]{:S(2)}, u32[]{:S(2)}) async-start(bf16[16,16,4224]{2,1,0:T(8,128)(2,1)} %bitcast.37), calls=%async_computation | async-start | bytes 4325376 | tf_op jit(solution)/shard_map/all_to_all | solution.py:285
  179.9 2.5 %shard_map.122 = (f32[32,4096]{1,0:T(8,128)S(1)}, f32[32,128]{1,0:T(8,128)S(1)}) custom-call(bf16[32,4096]{1,0:T(8,128)(2,1)S(1)} %get-tuple-element.14.q_ref, bf16[1024,512]{1,0:T(8,128)(2,1)S(1)} %bitcast.27, bf16[1024,512]{1,0:T(8,128)(2,1)S(1)} %bitcast.29, bf16[64,512]{1,0:T(8,128)(2,1)S(1)} %bitcast.33, bf16[64,512]{1,0:T(8,128)(2,1)S(1)} %bitcast.35, ...), custom_call_target="tpu_custom_call" | custom-call | flops 536870912 | bytes 2097152 | tf_op jit(solution)/shard_map/pallas_call | solution.py:131
  182.4 2.5 %shard_map.119 = (f32[32,4096]{1,0:T(8,128)S(1)}, f32[32,128]{1,0:T(8,128)S(1)}) custom-call(bf16[32,4096]{1,0:T(8,128)(2,1)S(1)} %get-tuple-element.13.q_ref, bf16[1024,512]{1,0:T(8,128)(2,1)S(1)} %bitcast.28, bf16[1024,512]{1,0:T(8,128)(2,1)S(1)} %bitcast.30, bf16[64,512]{1,0:T(8,128)(2,1)S(1)} %bitcast.34, bf16[64,512]{1,0:T(8,128)(2,1)S(1)} %bitcast.36, ...), custom_call_target="tpu_custom_call" | custom-call | flops 536870912 | bytes 2097152 | tf_op jit(solution)/shard_map/pallas_call | solution.py:131
  184.9 7.6 %shard_map.123 = bf16[32,4096]{1,0:T(8,128)(2,1)S(1)} custom-call(bf16[256,4224]{1,0:T(8,128)(2,1)S(1)} %bitcast.26, bf16[32,256]{1,0:T(8,128)(2,1)S(1)} %convert_element_type.20.place_ref, f32[32,4096]{1,0:T(8,128)S(1)} %get-tuple-element.11.own_ref, f32[32,128]{1,0:T(8,128)S(1)} %get-tuple-element.12.level_ref), custom_call_target="tpu_custom_call" | custom-call | flops 67108864 | bytes 2162688 | tf_op jit(solution)/shard_map/pallas_call | solution.py:170
  192.5 33.5 %all-to-all-done = bf16[16,16,4224]{2,1,0:T(8,128)(2,1)} async-done(((bf16[16,16,4224]{2,1,0:T(8,128)(2,1)}), bf16[16,16,4224]{2,1,0:T(8,128)(2,1)}, u32[]{:S(2)}, u32[]{:S(2)}) %all-to-all-start) | async-done | bytes 2162720 | tf_op jit(solution)/shard_map/all_to_all | solution.py:285
  225.9 9.2 %shard_map.120 = bf16[32,4096]{1,0:T(8,128)(2,1)S(1)} custom-call(bf16[256,4224]{1,0:T(8,128)(2,1)} %bitcast.2.back_ref, bf16[32,256]{1,0:T(8,128)(2,1)S(1)} %convert_element_type.20.place_ref, f32[32,4096]{1,0:T(8,128)S(1)} %get-tuple-element.9.own_ref, f32[32,128]{1,0:T(8,128)S(1)} %get-tuple-element.10.level_ref), custom_call_target="tpu_custom_call" | custom-call | flops 67108864 | bytes 2162688 | tf_op jit(solution)/shard_map/pallas_call | solution.py:170
  (68 shorter events, 23.5 us)
Async XLA Ops:
  1.1 7.2 %collective-permute-start.4 = (bf16[32,4096]{1,0:T(8,128)(2,1)S(1)}, bf16[32,4096]{1,0:T(8,128)(2,1)S(1)}, u32[]{:S(2)}, u32[]{:S(2)}) collective-permute-start(bf16[32,4096]{1,0:T(8,128)(2,1)S(1)} %get-tuple-element.14.q_ref), channel_id=1, source_target_pairs={{0,2},{1,3},{2,0},{3,1},{4,6},{5,7},{6,4},{7,5},{8,10},{9,11},{10,... | collective-permute-start | bytes 786440 | tf_op jit(solution)/shard_map/ppermute | solution.py:191
  1.4 74.8 %collective-permute-start = (bf16[32,4096]{1,0:T(8,128)(2,1)S(1)}, bf16[32,4096]{1,0:T(8,128)(2,1)S(1)}, u32[]{:S(2)}, u32[]{:S(2)}) collective-permute-start(bf16[32,4096]{1,0:T(8,128)(2,1)S(1)} %get-tuple-element.13.q_ref), channel_id=1, source_target_pairs={{0,8},{1,9},{2,10},{3,11},{4,12},{5,13},{6,14},{7,15},{8,0},{9,1},... | collective-permute-start | bytes 786440 | tf_op jit(solution)/shard_map/ppermute | solution.py:191
  8.3 29.4 %collective-permute-start.5 = (bf16[64,4096]{1,0:T(8,128)(2,1)S(1)}, bf16[64,4096]{1,0:T(8,128)(2,1)S(1)}, u32[]{:S(2)}, u32[]{:S(2)}) collective-permute-start(bf16[64,4096]{1,0:T(8,128)(2,1)S(1)} %pad_maximum_fusion.5), channel_id=1, source_target_pairs={{0,8},{1,9},{2,10},{3,11},{4,12},{5,13},{6,14},{7,15},{8,0},{9,1},... | collective-permute-start | bytes 1572872 | tf_op jit(solution)/shard_map/ppermute | solution.py:191
  38.8 41.2 %collective-permute-start.6 = (bf16[128,4096]{1,0:T(8,128)(2,1)}, bf16[128,4096]{1,0:T(8,128)(2,1)S(1)}, u32[]{:S(2)}, u32[]{:S(2)}) collective-permute-start(bf16[128,4096]{1,0:T(8,128)(2,1)} %pad_maximum_fusion.3), channel_id=1, source_target_pairs={{0,4},{1,5},{2,6},{3,7},{4,0},{5,1},{6,2},{7,3},{8,12},{9,13},{10,... | collective-permute-start | bytes 3145736 | tf_op jit(solution)/shard_map/ppermute | solution.py:191
  77.1 15.4 %collective-permute-start.1 = (bf16[64,4096]{1,0:T(8,128)(2,1)}, bf16[64,4096]{1,0:T(8,128)(2,1)S(1)}, u32[]{:S(2)}, u32[]{:S(2)}) collective-permute-start(bf16[64,4096]{1,0:T(8,128)(2,1)} %pad_maximum_fusion.4), channel_id=1, source_target_pairs={{0,4},{1,5},{2,6},{3,7},{4,0},{5,1},{6,2},{7,3},{8,12},{9,13},{10,... | collective-permute-start | bytes 1572872 | tf_op jit(solution)/shard_map/ppermute | solution.py:191
  81.5 15.4 %collective-permute-start.7 = (bf16[256,4096]{1,0:T(8,128)(2,1)}, bf16[256,4096]{1,0:T(8,128)(2,1)}, u32[]{:S(2)}, u32[]{:S(2)}) collective-permute-start(bf16[256,4096]{1,0:T(8,128)(2,1)} %pad_maximum_fusion.1), channel_id=1, source_target_pairs={{0,1},{1,0},{2,3},{3,2},{4,5},{5,4},{6,7},{7,6},{8,9},{9,8},{10,11... | collective-permute-start | bytes 6291464 | tf_op jit(solution)/shard_map/ppermute | solution.py:191
  93.6 6.6 %copy-start.8 = (pred[256,512]{1,0:T(32,128)(4,1)S(1)}, pred[256,512]{1,0:T(32,128)(4,1)}, u32[]{:S(2)}) copy-start(pred[256,512]{1,0:T(32,128)(4,1)} %and.137) | copy-start | bytes 393220
  93.6 29.7 %collective-permute-start.2 = (bf16[128,4096]{1,0:T(8,128)(2,1)}, bf16[128,4096]{1,0:T(8,128)(2,1)}, u32[]{:S(2)}, u32[]{:S(2)}) collective-permute-start(bf16[128,4096]{1,0:T(8,128)(2,1)} %pad_maximum_fusion.2), channel_id=1, source_target_pairs={{0,2},{1,3},{2,0},{3,1},{4,6},{5,7},{6,4},{7,5},{8,10},{9,11},{10,... | collective-permute-start | bytes 3145736 | tf_op jit(solution)/shard_map/ppermute | solution.py:191
  100.1 3.6 %copy-start.4 = (bf16[1024,512]{1,0:T(8,128)(2,1)S(1)}, bf16[1024,512]{1,0:T(8,128)(2,1)}, u32[]{:S(2)}) copy-start(bf16[1024,512]{1,0:T(8,128)(2,1)} %k_ref.3) | copy-start | bytes 3145732
  100.1 3.6 %copy-start.6 = (bf16[1024,512]{1,0:T(8,128)(2,1)S(1)}, bf16[1024,512]{1,0:T(8,128)(2,1)}, u32[]{:S(2)}) copy-start(bf16[1024,512]{1,0:T(8,128)(2,1)} %v_ref.3) | copy-start | bytes 3145732
  117.7 54.4 %all-to-all-start.1 = ((bf16[16,16,4224]{2,1,0:T(8,128)(2,1)}), bf16[16,16,4224]{2,1,0:T(8,128)(2,1)S(1)}, u32[]{:S(2)}, u32[]{:S(2)}) async-start(bf16[16,16,4224]{2,1,0:T(8,128)(2,1)} %bitcast.38), calls=%async_computation.1 | async-start | bytes 4325376 | tf_op jit(solution)/shard_map/all_to_all | solution.py:285
  126.1 6.9 %collective-permute-start.3 = (bf16[256,4096]{1,0:T(8,128)(2,1)}, bf16[256,4096]{1,0:T(8,128)(2,1)}, u32[]{:S(2)}, u32[]{:S(2)}) collective-permute-start(bf16[256,4096]{1,0:T(8,128)(2,1)} %pad_maximum_fusion), channel_id=1, source_target_pairs={{0,1},{1,0},{2,3},{3,2},{4,5},{5,4},{6,7},{7,6},{8,9},{9,8},{10,11... | collective-permute-start | bytes 6291464 | tf_op jit(solution)/shard_map/ppermute | solution.py:191
  129.1 7.0 %copy-start.9 = (pred[256,512]{1,0:T(32,128)(4,1)S(1)}, pred[256,512]{1,0:T(32,128)(4,1)}, u32[]{:S(2)}) copy-start(pred[256,512]{1,0:T(32,128)(4,1)} %and.127) | copy-start | bytes 393220
  136.1 3.6 %copy-start.5 = (bf16[1024,512]{1,0:T(8,128)(2,1)S(1)}, bf16[1024,512]{1,0:T(8,128)(2,1)}, u32[]{:S(2)}) copy-start(bf16[1024,512]{1,0:T(8,128)(2,1)} %k_ref.3) | copy-start | bytes 3145732
  136.1 3.6 %copy-start.7 = (bf16[1024,512]{1,0:T(8,128)(2,1)S(1)}, bf16[1024,512]{1,0:T(8,128)(2,1)}, u32[]{:S(2)}) copy-start(bf16[1024,512]{1,0:T(8,128)(2,1)} %v_ref.3) | copy-start | bytes 3145732
  153.6 23.7 %copy-start.10 = (s32[32]{0:T(128)S(1)}, s32[32]{0:T(128)}, u32[]{:S(2)}) copy-start(s32[32]{0:T(128)} %param.21) | copy-start | bytes 388
  153.6 23.8 %copy-start.2 = (bf16[2,32,512]{2,1,0:T(8,128)(2,1)S(1)}, bf16[2,32,512]{2,1,0:T(8,128)(2,1)}, u32[]{:S(2)}) copy-start(bf16[2,32,512]{2,1,0:T(8,128)(2,1)} %param.17) | copy-start | bytes 196612
  153.6 23.8 %copy-start.3 = (bf16[2,32,512]{2,1,0:T(8,128)(2,1)S(1)}, bf16[2,32,512]{2,1,0:T(8,128)(2,1)}, u32[]{:S(2)}) copy-start(bf16[2,32,512]{2,1,0:T(8,128)(2,1)} %param.18) | copy-start | bytes 196612
  172.1 53.8 %all-to-all-start = ((bf16[16,16,4224]{2,1,0:T(8,128)(2,1)}), bf16[16,16,4224]{2,1,0:T(8,128)(2,1)}, u32[]{:S(2)}, u32[]{:S(2)}) async-start(bf16[16,16,4224]{2,1,0:T(8,128)(2,1)} %bitcast.37), calls=%async_computation | async-start | bytes 4325376 | tf_op jit(solution)/shard_map/all_to_all | solution.py:285
  177.5 1.2 copy-start
  178.7 1.2 copy-start.1

commit v3 on v2

--- a/solution.py
+++ b/solution.py
@@ -244,16 +244,24 @@
         lax.all_to_all, axis_name="kv", split_axis=0, concat_axis=0, tiled=True
     )
     received, owns, backs = [], [], []
-    if 4 * capacity >= rows and devices & (devices - 1) == 0:
+    if 4 * capacity >= rows and devices & (devices - 1) == 0 and max(devices, capacity) <= 256:
         me = lax.axis_index("kv")
-        everyone = lax.all_gather(slot_index, "kv", axis=0)
-        wanted = me * capacity + jnp.arange(capacity, dtype=jnp.int32)
-        filled = jnp.any(everyone[:, None, :, :] == wanted[None, :, None, None], axis=3)
+        labels = jnp.concatenate([target.reshape(rows, path), rank.reshape(rows, path)], axis=1)
+        labels = jnp.pad(labels, ((0, 0), (0, LANES - 2 * path))).astype(jnp.bfloat16)
+        ranks = jnp.arange(capacity, dtype=jnp.int32)[None, :, None, None]
         for t in range(steps):
-            order, gathered = gather_rows(queries[t], devices, exchange_masks(devices, t))
+            order, gathered = gather_rows(
+                jnp.concatenate([queries[t], labels], axis=1),
+                devices,
+                exchange_masks(devices, t),
+            )
+            named = gathered[:, WIDTH : WIDTH + 2 * path].astype(jnp.int32)
+            named = named.reshape(devices, 1, rows, 2 * path)
+            filled = jnp.any((named[..., :path] == me) & (named[..., path:] == ranks), axis=3)
             sender = jnp.asarray(order, jnp.int32) ^ me
             chosen = (
-                filled[:, :, None, :] & (device_ids[:, None] == sender[None, :])[:, None, :, None]
+                filled.transpose(1, 0, 2)[None]
+                & (device_ids[:, None] == sender[None, :])[:, None, :, None]
             ).astype(jnp.bfloat16)
             received.append(
                 jnp.dot(

time: 237 us -> 224 us (0.945)
  waiting for transfers between devices: 84.8 us -> 124 us
  blocking collectives: 37 us -> 0 us
  local copies, waits for them, and re-layouts: 24.7 us -> 13.9 us
  other arithmetic: 11.8 us -> 4.7 us
  matrix products: 7.18 us -> 10.2 us
    all_gather x1 -> x0, blocking collectives: 37 us -> none  [per_device(): everyone = lax.all_gather(slot_index, 'kv', axis=0)]
    ppermute x8, waiting for transfers between devices: 32.8 us -> 64.7 us  [gather_rows(): partner = lax.ppermute(held, 'kv', [(i, i ^ mask) for i in range(devices)])]
    all_to_all x2, waiting for transfers between devices: 51.9 us -> 59.7 us  [per_device(): backs.append(exchange(result.reshape(devices, capacity, WIDTH + LANES)))]
    concatenate x6 -> x3, other arithmetic: 7.4 us -> 0.71 us  [gather_rows(): held = jnp.concatenate([held, partner], axis=0)]
    concatenate x2, local copies, waits for them, and re-layouts: 6.28 us -> 0.57 us  [gather_rows(): held = jnp.concatenate([held, partner], axis=0)]
    and x2 -> x4, local copies, waits for them, and re-layouts: 5.3 us -> 2.11 us  [the longest x2 1.75 us: per_device(): filled.transpose(1, 0, 2)[None]]
    dot_general x2, matrix products: 7.18 us -> 10.2 us  [per_device(): jnp.dot(chosen.reshape(slots_all, devices * rows), gathered, preferred_el...]
    unnamed x30 -> x43, local copies, waits for them, and re-layouts: 11.6 us -> 9.01 us
  transfers between devices with their start and end apart: 10 -> 10, of which waited for: 5 -> 8; matrix products, arithmetic and copies ran while one was open for 17% -> 4% of each run, Pallas kernels for 17% -> 12%
where the time goes in v3:
time: 224 us; the launch traced here: 223 us
  waiting for transfers between devices  124 us (55%)
  Pallas kernels  50.1 us (22%)
  starting transfers between devices  19.7 us (9%)
  local copies, waits for them, and re-layouts  13.9 us (6%)
  matrix products  10.2 us (5%)
  other arithmetic  4.7 us (2%)
    ppermute x8, waiting for transfers between devices, gather_rows(): partner = lax.ppermute(held, 'kv', [(i, i ^ mask) for i in range(devices)])  64.7 us
    all_to_all x2, waiting for transfers between devices, per_device(): backs.append(exchange(result.reshape(devices, capacity, WIDTH + LANES)))  59.7 us
    pallas_call x2, Pallas kernels, attend(): pl.pallas_call(attend_kernel, grid=(count // tile,), in_specs=[pl.BlockSp...  28.4 us
    pallas_call x2, Pallas kernels, merge(): pl.pallas_call(merge_kernel, out_shape=jax.ShapeDtypeStruct(own.shape, jn...  16.8 us
    all_to_all x2, starting transfers between devices, per_device(): backs.append(exchange(result.reshape(devices, capacity, WIDTH + LANES)))  11.1 us
    dot_general x2, matrix products, per_device(): jnp.dot(chosen.reshape(slots_all, devices * rows), gathered, preferred_el...  10.2 us
    unnamed x43, local copies, waits for them, and re-layouts  9.01 us
    ppermute x8, starting transfers between devices, gather_rows(): partner = lax.ppermute(held, 'kv', [(i, i ^ mask) for i in range(devices)])  8.55 us
  transfers between devices with their start and end apart: 10, of which 8 were waited for; matrix products, arithmetic and copies ran while one was open for 4% of the time, Pallas kernels for 12%

profile of v3, /device:TPU:11, one launch (start us, length us, event | category | flops | bytes accessed | tf_op | source)
XLA Modules:
  0.0 223.5 jit_solution(3517687273074084384)
XLA Ops:
  4.1 2.3 %collective-permute-start = (bf16[32,4224]{1,0:T(8,128)(2,1)S(1)}, bf16[32,4224]{1,0:T(8,128)(2,1)S(1)}, u32[]{:S(2)}, u32[]{:S(2)}) collective-permute-start(bf16[32,4224]{1,0:T(8,128)(2,1)S(1)} %get-tuple-element.15), channel_id=1, source_target_pairs={{0,8},{1,9},{2,10},{3,11},{4,12},{5,13},{6,14},{7,15},{8,0},{9,1},... | collective-permute-start | bytes 811016 | tf_op jit(solution)/shard_map/ppermute | solution.py:191
  6.7 11.6 %collective-permute-done = bf16[32,4224]{1,0:T(8,128)(2,1)S(1)} collective-permute-done((bf16[32,4224]{1,0:T(8,128)(2,1)S(1)}, bf16[32,4224]{1,0:T(8,128)(2,1)S(1)}, u32[]{:S(2)}, u32[]{:S(2)}) %collective-permute-start) | collective-permute-done | bytes 270368 | tf_op jit(solution)/shard_map/ppermute | solution.py:191
  18.5 3.1 %collective-permute-start.5 = (bf16[64,4224]{1,0:T(8,128)(2,1)S(1)}, bf16[64,4224]{1,0:T(8,128)(2,1)S(1)}, u32[]{:S(2)}, u32[]{:S(2)}) collective-permute-start(bf16[64,4224]{1,0:T(8,128)(2,1)S(1)} %get-tuple-element.24), channel_id=1, source_target_pairs={{0,8},{1,9},{2,10},{3,11},{4,12},{5,13},{6,14},{7,15},{8,0},{9,1},... | collective-permute-start | bytes 1622024 | tf_op jit(solution)/shard_map/ppermute | solution.py:191
  21.7 18.2 %collective-permute-done.1 = bf16[64,4224]{1,0:T(8,128)(2,1)S(1)} collective-permute-done((bf16[64,4224]{1,0:T(8,128)(2,1)S(1)}, bf16[64,4224]{1,0:T(8,128)(2,1)S(1)}, u32[]{:S(2)}, u32[]{:S(2)}) %collective-permute-start.1) | collective-permute-done | bytes 540704 | tf_op jit(solution)/shard_map/ppermute | solution.py:191
  39.9 5.5 %collective-permute-done.5 = bf16[64,4224]{1,0:T(8,128)(2,1)S(1)} collective-permute-done((bf16[64,4224]{1,0:T(8,128)(2,1)S(1)}, bf16[64,4224]{1,0:T(8,128)(2,1)S(1)}, u32[]{:S(2)}, u32[]{:S(2)}) %collective-permute-start.5) | collective-permute-done | bytes 540704 | tf_op jit(solution)/shard_map/ppermute | solution.py:191
  46.7 23.2 %collective-permute-done.2 = bf16[128,4224]{1,0:T(8,128)(2,1)S(1)} collective-permute-done((bf16[128,4224]{1,0:T(8,128)(2,1)S(1)}, bf16[128,4224]{1,0:T(8,128)(2,1)S(1)}, u32[]{:S(2)}, u32[]{:S(2)}) %collective-permute-start.2) | collective-permute-done | bytes 1081376 | tf_op jit(solution)/shard_map/ppermute | solution.py:191
  70.4 2.3 %collective-permute-start.3 = (bf16[256,4224]{1,0:T(8,128)(2,1)S(1)}, bf16[256,4224]{1,0:T(8,128)(2,1)S(1)}, u32[]{:S(2)}, u32[]{:S(2)}) collective-permute-start(bf16[256,4224]{1,0:T(8,128)(2,1)S(1)} %get-tuple-element.19), channel_id=1, source_target_pairs={{0,1},{1,0},{2,3},{3,2},{4,5},{5,4},{6,7},{7,6},{8,9},{9,8},{10,11... | collective-permute-start | bytes 6488072 | tf_op jit(solution)/shard_map/ppermute | solution.py:191
  73.2 3.4 %collective-permute-done.3 = bf16[256,4224]{1,0:T(8,128)(2,1)S(1)} collective-permute-done((bf16[256,4224]{1,0:T(8,128)(2,1)S(1)}, bf16[256,4224]{1,0:T(8,128)(2,1)S(1)}, u32[]{:S(2)}, u32[]{:S(2)}) %collective-permute-start.3) | collective-permute-done | bytes 2162720 | tf_op jit(solution)/shard_map/ppermute | solution.py:191
  76.9 2.7 %collective-permute-done.7 = bf16[256,4224]{1,0:T(8,128)(2,1)S(1)} collective-permute-done((bf16[256,4224]{1,0:T(8,128)(2,1)S(1)}, bf16[256,4224]{1,0:T(8,128)(2,1)S(1)}, u32[]{:S(2)}, u32[]{:S(2)}) %collective-permute-start.7) | collective-permute-done | bytes 2162720 | tf_op jit(solution)/shard_map/ppermute | solution.py:191
  80.2 1.9 copy-done.11
  83.8 5.1 %convolution_convert_fusion.q_ref = bf16[256,4224]{1,0:T(8,128)(2,1)} fusion(pred[256,512]{1,0:T(32,128)(4,1)S(1)} %and.166, bf16[512,4224]{1,0:T(8,128)(2,1)} %copy-done.11), kind=kOutput, calls=%fused_computation | convolution fusion | flops 1108377600 | bytes 6619136 | tf_op jit(solution)/shard_map/dot_general | solution.py:267
  88.9 14.2 %shard_map.121 = bf16[256,4224]{1,0:T(8,128)(2,1)S(1)} custom-call(bf16[256,4224]{1,0:T(8,128)(2,1)} %convolution_convert_fusion.q_ref, bf16[1024,512]{1,0:T(8,128)(2,1)S(1)} %copy-done.6, bf16[1024,512]{1,0:T(8,128)(2,1)S(1)} %copy-done.8), custom_call_target="tpu_custom_call" | custom-call | flops 4294967296 | bytes 6291456 | tf_op jit(solution)/shard_map/pallas_call | solution.py:74
  103.1 1.4 copy-done.3
  104.5 6.1 %all-to-all-start.1 = ((bf16[16,16,4224]{2,1,0:T(8,128)(2,1)}), bf16[16,16,4224]{2,1,0:T(8,128)(2,1)S(1)}, u32[]{:S(2)}, u32[]{:S(2)}) async-start(bf16[16,16,4224]{2,1,0:T(8,128)(2,1)} %bitcast.42), calls=%async_computation.1 | async-start | bytes 4325376 | tf_op jit(solution)/shard_map/all_to_all | solution.py:293
  112.5 5.1 %convolution_convert_fusion.1.q_ref = bf16[256,4224]{1,0:T(8,128)(2,1)} fusion(pred[256,512]{1,0:T(32,128)(4,1)S(1)} %and.152, bf16[512,4224]{1,0:T(8,128)(2,1)} %copy-done.12), kind=kOutput, calls=%fused_computation.1 | convolution fusion | flops 1108377600 | bytes 6619136 | tf_op jit(solution)/shard_map/dot_general | solution.py:267
  117.6 14.2 %shard_map.118 = bf16[256,4224]{1,0:T(8,128)(2,1)S(1)} custom-call(bf16[256,4224]{1,0:T(8,128)(2,1)} %convolution_convert_fusion.1.q_ref, bf16[1024,512]{1,0:T(8,128)(2,1)S(1)} %copy-done.7, bf16[1024,512]{1,0:T(8,128)(2,1)S(1)} %copy-done.9), custom_call_target="tpu_custom_call" | custom-call | flops 4294967296 | bytes 6291456 | tf_op jit(solution)/shard_map/pallas_call | solution.py:74
  131.8 1.4 copy-done.2
  133.1 26.3 %all-to-all-done.1 = bf16[16,16,4224]{2,1,0:T(8,128)(2,1)S(1)} async-done(((bf16[16,16,4224]{2,1,0:T(8,128)(2,1)}), bf16[16,16,4224]{2,1,0:T(8,128)(2,1)S(1)}, u32[]{:S(2)}, u32[]{:S(2)}) %all-to-all-start.1) | async-done | bytes 2162720 | tf_op jit(solution)/shard_map/all_to_all | solution.py:293
  159.4 5.0 %all-to-all-start = ((bf16[16,16,4224]{2,1,0:T(8,128)(2,1)}), bf16[16,16,4224]{2,1,0:T(8,128)(2,1)}, u32[]{:S(2)}, u32[]{:S(2)}) async-start(bf16[16,16,4224]{2,1,0:T(8,128)(2,1)} %bitcast.41), calls=%async_computation | async-start | bytes 4325376 | tf_op jit(solution)/shard_map/all_to_all | solution.py:293
  167.4 2.5 %shard_map.119 = (f32[32,4096]{1,0:T(8,128)S(1)}, f32[32,128]{1,0:T(8,128)S(1)}) custom-call(bf16[32,4096]{1,0:T(8,128)(2,1)S(1)} %get-tuple-element.13.q_ref, bf16[1024,512]{1,0:T(8,128)(2,1)S(1)} %bitcast.37, bf16[1024,512]{1,0:T(8,128)(2,1)S(1)} %bitcast.39, bf16[64,512]{1,0:T(8,128)(2,1)S(1)} %bitcast.45, bf16[64,512]{1,0:T(8,128)(2,1)S(1)} %bitcast.47, ...), custom_call_target="tpu_custom_call" | custom-call | flops 536870912 | bytes 2097152 | tf_op jit(solution)/shard_map/pallas_call | solution.py:131
  169.9 2.5 %shard_map.122 = (f32[32,4096]{1,0:T(8,128)S(1)}, f32[32,128]{1,0:T(8,128)S(1)}) custom-call(bf16[32,4096]{1,0:T(8,128)(2,1)S(1)} %get-tuple-element.14.q_ref, bf16[1024,512]{1,0:T(8,128)(2,1)S(1)} %bitcast.38, bf16[1024,512]{1,0:T(8,128)(2,1)S(1)} %bitcast.40, bf16[64,512]{1,0:T(8,128)(2,1)S(1)} %bitcast.46, bf16[64,512]{1,0:T(8,128)(2,1)S(1)} %bitcast.48, ...), custom_call_target="tpu_custom_call" | custom-call | flops 536870912 | bytes 2097152 | tf_op jit(solution)/shard_map/pallas_call | solution.py:131
  172.3 7.6 %shard_map.123 = bf16[32,4096]{1,0:T(8,128)(2,1)S(1)} custom-call(bf16[256,4224]{1,0:T(8,128)(2,1)S(1)} %bitcast.36, bf16[32,256]{1,0:T(8,128)(2,1)S(1)} %convert_element_type.23.place_ref, f32[32,4096]{1,0:T(8,128)S(1)} %get-tuple-element.11.own_ref, f32[32,128]{1,0:T(8,128)S(1)} %get-tuple-element.12.level_ref), custom_call_target="tpu_custom_call" | custom-call | flops 67108864 | bytes 2162688 | tf_op jit(solution)/shard_map/pallas_call | solution.py:170
  179.9 33.5 %all-to-all-done = bf16[16,16,4224]{2,1,0:T(8,128)(2,1)} async-done(((bf16[16,16,4224]{2,1,0:T(8,128)(2,1)}), bf16[16,16,4224]{2,1,0:T(8,128)(2,1)}, u32[]{:S(2)}, u32[]{:S(2)}) %all-to-all-start) | async-done | bytes 2162720 | tf_op jit(solution)/shard_map/all_to_all | solution.py:293
  213.4 9.2 %shard_map.120 = bf16[32,4096]{1,0:T(8,128)(2,1)S(1)} custom-call(bf16[256,4224]{1,0:T(8,128)(2,1)} %bitcast.7.back_ref, bf16[32,256]{1,0:T(8,128)(2,1)S(1)} %convert_element_type.23.place_ref, f32[32,4096]{1,0:T(8,128)S(1)} %get-tuple-element.9.own_ref, f32[32,128]{1,0:T(8,128)S(1)} %get-tuple-element.10.level_ref), custom_call_target="tpu_custom_call" | custom-call | flops 67108864 | bytes 2162688 | tf_op jit(solution)/shard_map/pallas_call | solution.py:170
  (94 shorter events, 14.8 us)
Async XLA Ops:
  3.1 18.5 %copy-start.14 = (s32[16]{0:T(128)S(1)}, s32[16]{0:T(128)}, u32[]{:S(2)}) copy-start(s32[16]{0:T(128)} %constant.80.clone) | copy-start | bytes 196
  3.1 18.5 %copy-start.15 = (s32[16]{0:T(128)S(1)}, s32[16]{0:T(128)}, u32[]{:S(2)}) copy-start(s32[16]{0:T(128)} %constant.79.clone) | copy-start | bytes 196
  4.1 14.2 %collective-permute-start = (bf16[32,4224]{1,0:T(8,128)(2,1)S(1)}, bf16[32,4224]{1,0:T(8,128)(2,1)S(1)}, u32[]{:S(2)}, u32[]{:S(2)}) collective-permute-start(bf16[32,4224]{1,0:T(8,128)(2,1)S(1)} %get-tuple-element.15), channel_id=1, source_target_pairs={{0,8},{1,9},{2,10},{3,11},{4,12},{5,13},{6,14},{7,15},{8,0},{9,1},... | collective-permute-start | bytes 811016 | tf_op jit(solution)/shard_map/ppermute | solution.py:191
  6.4 11.9 %collective-permute-start.4 = (bf16[32,4224]{1,0:T(8,128)(2,1)S(1)}, bf16[32,4224]{1,0:T(8,128)(2,1)S(1)}, u32[]{:S(2)}, u32[]{:S(2)}) collective-permute-start(bf16[32,4224]{1,0:T(8,128)(2,1)S(1)} %get-tuple-element.26), channel_id=1, source_target_pairs={{0,2},{1,3},{2,0},{3,1},{4,6},{5,7},{6,4},{7,5},{8,10},{9,11},{10,... | collective-permute-start | bytes 811016 | tf_op jit(solution)/shard_map/ppermute | solution.py:191
  18.4 21.5 %collective-permute-start.1 = (bf16[64,4224]{1,0:T(8,128)(2,1)S(1)}, bf16[64,4224]{1,0:T(8,128)(2,1)S(1)}, u32[]{:S(2)}, u32[]{:S(2)}) collective-permute-start(bf16[64,4224]{1,0:T(8,128)(2,1)S(1)} %get-tuple-element.23), channel_id=1, source_target_pairs={{0,4},{1,5},{2,6},{3,7},{4,0},{5,1},{6,2},{7,3},{8,12},{9,13},{10,... | collective-permute-start | bytes 1622024 | tf_op jit(solution)/shard_map/ppermute | solution.py:191
  18.5 26.9 %collective-permute-start.5 = (bf16[64,4224]{1,0:T(8,128)(2,1)S(1)}, bf16[64,4224]{1,0:T(8,128)(2,1)S(1)}, u32[]{:S(2)}, u32[]{:S(2)}) collective-permute-start(bf16[64,4224]{1,0:T(8,128)(2,1)S(1)} %get-tuple-element.24), channel_id=1, source_target_pairs={{0,8},{1,9},{2,10},{3,11},{4,12},{5,13},{6,14},{7,15},{8,0},{9,1},... | collective-permute-start | bytes 1622024 | tf_op jit(solution)/shard_map/ppermute | solution.py:191
  21.7 25.0 %copy-start.10 = (bf16[512,4224]{1,0:T(8,128)(2,1)S(1)}, bf16[512,4224]{1,0:T(8,128)(2,1)}, u32[]{:S(2)}) copy-start(bf16[512,4224]{1,0:T(8,128)(2,1)} %get-tuple-element.25) | copy-start | bytes 12976132
  45.6 24.3 %collective-permute-start.2 = (bf16[128,4224]{1,0:T(8,128)(2,1)S(1)}, bf16[128,4224]{1,0:T(8,128)(2,1)S(1)}, u32[]{:S(2)}, u32[]{:S(2)}) collective-permute-start(bf16[128,4224]{1,0:T(8,128)(2,1)S(1)} %get-tuple-element.21), channel_id=1, source_target_pairs={{0,2},{1,3},{2,0},{3,1},{4,6},{5,7},{6,4},{7,5},{8,10},{9,11},{10,... | collective-permute-start | bytes 3244040 | tf_op jit(solution)/shard_map/ppermute | solution.py:191
  45.9 24.0 %collective-permute-start.6 = (bf16[128,4224]{1,0:T(8,128)(2,1)S(1)}, bf16[128,4224]{1,0:T(8,128)(2,1)S(1)}, u32[]{:S(2)}, u32[]{:S(2)}) collective-permute-start(bf16[128,4224]{1,0:T(8,128)(2,1)S(1)} %get-tuple-element.22), channel_id=1, source_target_pairs={{0,4},{1,5},{2,6},{3,7},{4,0},{5,1},{6,2},{7,3},{8,12},{9,13},{10,... | collective-permute-start | bytes 3244040 | tf_op jit(solution)/shard_map/ppermute | solution.py:191
  46.6 26.1 %slice-start = ((s8[4325376]{0:T(1024)(128)(4,1)}), s8[4194304]{0:T(1024)(128)(4,1)S(1)}, s32[]{:S(2)}) async-start(s8[4325376]{0:T(1024)(128)(4,1)} %bitcast.53), calls=%async_computation.2 | async-start | bytes 8388608
  46.7 26.0 %slice-start.1 = ((s8[4325376]{0:T(1024)(128)(4,1)}), s8[131072]{0:T(1024)(128)(4,1)S(1)}, s32[]{:S(2)}) async-start(s8[4325376]{0:T(1024)(128)(4,1)} %bitcast.53), calls=%async_computation.3 | async-start | bytes 262144
  70.4 6.2 %collective-permute-start.3 = (bf16[256,4224]{1,0:T(8,128)(2,1)S(1)}, bf16[256,4224]{1,0:T(8,128)(2,1)S(1)}, u32[]{:S(2)}, u32[]{:S(2)}) collective-permute-start(bf16[256,4224]{1,0:T(8,128)(2,1)S(1)} %get-tuple-element.19), channel_id=1, source_target_pairs={{0,1},{1,0},{2,3},{3,2},{4,5},{5,4},{6,7},{7,6},{8,9},{9,8},{10,11... | collective-permute-start | bytes 6488072 | tf_op jit(solution)/shard_map/ppermute | solution.py:191
  72.8 6.9 %collective-permute-start.7 = (bf16[256,4224]{1,0:T(8,128)(2,1)S(1)}, bf16[256,4224]{1,0:T(8,128)(2,1)S(1)}, u32[]{:S(2)}, u32[]{:S(2)}) collective-permute-start(bf16[256,4224]{1,0:T(8,128)(2,1)S(1)} %get-tuple-element.20), channel_id=1, source_target_pairs={{0,1},{1,0},{2,3},{3,2},{4,5},{5,4},{6,7},{7,6},{8,9},{9,8},{10,11... | collective-permute-start | bytes 6488072 | tf_op jit(solution)/shard_map/ppermute | solution.py:191
  76.9 3.1 %copy-start.12 = (bf16[512,4224]{1,0:T(8,128)(2,1)}, bf16[512,4224]{1,0:T(8,128)(2,1)S(1)}, u32[]{:S(2)}) copy-start(bf16[512,4224]{1,0:T(8,128)(2,1)S(1)} %constant_dynamic-update-slice_fusion) | copy-start | bytes 12976132
  80.0 2.1 copy-start.11
  83.8 5.1 %copy-start.6 = (bf16[1024,512]{1,0:T(8,128)(2,1)S(1)}, bf16[1024,512]{1,0:T(8,128)(2,1)}, u32[]{:S(2)}) copy-start(bf16[1024,512]{1,0:T(8,128)(2,1)} %k_ref.3) | copy-start | bytes 3145732
  83.8 5.1 %copy-start.8 = (bf16[1024,512]{1,0:T(8,128)(2,1)S(1)}, bf16[1024,512]{1,0:T(8,128)(2,1)}, u32[]{:S(2)}) copy-start(bf16[1024,512]{1,0:T(8,128)(2,1)} %v_ref.3) | copy-start | bytes 3145732
  104.5 54.9 %all-to-all-start.1 = ((bf16[16,16,4224]{2,1,0:T(8,128)(2,1)}), bf16[16,16,4224]{2,1,0:T(8,128)(2,1)S(1)}, u32[]{:S(2)}, u32[]{:S(2)}) async-start(bf16[16,16,4224]{2,1,0:T(8,128)(2,1)} %bitcast.42), calls=%async_computation.1 | async-start | bytes 4325376 | tf_op jit(solution)/shard_map/all_to_all | solution.py:293
  112.4 5.1 %copy-start.7 = (bf16[1024,512]{1,0:T(8,128)(2,1)S(1)}, bf16[1024,512]{1,0:T(8,128)(2,1)}, u32[]{:S(2)}) copy-start(bf16[1024,512]{1,0:T(8,128)(2,1)} %k_ref.3) | copy-start | bytes 3145732
  112.5 5.1 %copy-start.9 = (bf16[1024,512]{1,0:T(8,128)(2,1)S(1)}, bf16[1024,512]{1,0:T(8,128)(2,1)}, u32[]{:S(2)}) copy-start(bf16[1024,512]{1,0:T(8,128)(2,1)} %v_ref.3) | copy-start | bytes 3145732
  159.4 5.4 %copy-start.13 = (s32[32]{0:T(128)S(1)}, s32[32]{0:T(128)}, u32[]{:S(2)}) copy-start(s32[32]{0:T(128)} %param.21) | copy-start | bytes 388
  159.4 5.5 %copy-start.4 = (bf16[2,32,512]{2,1,0:T(8,128)(2,1)S(1)}, bf16[2,32,512]{2,1,0:T(8,128)(2,1)}, u32[]{:S(2)}) copy-start(bf16[2,32,512]{2,1,0:T(8,128)(2,1)} %param.17) | copy-start | bytes 196612
  159.4 5.5 %copy-start.5 = (bf16[2,32,512]{2,1,0:T(8,128)(2,1)S(1)}, bf16[2,32,512]{2,1,0:T(8,128)(2,1)}, u32[]{:S(2)}) copy-start(bf16[2,32,512]{2,1,0:T(8,128)(2,1)} %param.18) | copy-start | bytes 196612
  159.4 54.0 %all-to-all-start = ((bf16[16,16,4224]{2,1,0:T(8,128)(2,1)}), bf16[16,16,4224]{2,1,0:T(8,128)(2,1)}, u32[]{:S(2)}, u32[]{:S(2)}) async-start(bf16[16,16,4224]{2,1,0:T(8,128)(2,1)} %bitcast.41), calls=%async_computation | async-start | bytes 4325376 | tf_op jit(solution)/shard_map/all_to_all | solution.py:293
  (4 other events, 5.2 us)
